TPU v7x, 128 devices: a whole 4x4x4 slice. The times are simulated.
128 devices in a mesh: fsdp: 8 (over x, z_hi), tp: 16 (over y, z_lo, core).
Axes of the slice: x: 4, y: 4, z: 4 (z_hi: 2, z_lo: 2; z = z_hi * 2 + z_lo), core: 2. Of those that a mesh axis runs over, the one named last changes fastest.
Arguments:
- hidden_in: bfloat16 [4096, 8192], P('fsdp'), may hold values from -100 to 100
- lengths: int32 [8, 8], P('fsdp'), may hold values from 1 to 256, 512 in all within a row
- norm_gain: float32 [8192], replicated, may hold values from 0.5 to 4
- query_weight: bfloat16 [8192, 8192], P(('fsdp', 'tp')), may hold values from -0.088388348 to 0.088388348
- key_weight: bfloat16 [8192, 1024], P(('fsdp', 'tp')), may hold values from -0.088388348 to 0.088388348
- value_weight: bfloat16 [8192, 1024], P(('fsdp', 'tp')), may hold values from -0.0625 to 0.0625
- out_weight: bfloat16 [8192, 8192], P(None, ('fsdp', 'tp')), may hold values from -0.0625 to 0.0625
- query_scale: float32 [8192], replicated, may hold values from 2.2097087e-05 to 0.00022097086
- key_scale: float32 [1024], replicated, may hold values from 2.2097087e-05 to 0.00022097086
- value_scale: float32 [1024], replicated, may hold values from 2.2097087e-05 to 0.00022097086
- out_scale: float32 [8192], replicated, may hold values from 2.2097087e-05 to 0.00022097086
Outputs:
- layer_out: bfloat16 [4096, 8192], P(('fsdp', 'tp'))
Inputs may be any that keep to these rules, and one draw needn't show every extreme that they name: `lengths`: each row sums to 512, and its largest entry is exactly 256.
All inputs are finite; a program needn't handle non-finite values.
Results may differ from a plain program's by a relative error of at most 0.024.
Values may be sent and summed in bfloat16 or wider, within the bound.
A program may use at most 128 MiB of HBM per device.

v0:
```python
import math

import jax
import jax.numpy as jnp
from jax import lax
from jax.sharding import PartitionSpec as P

KV = 8
HD = 128


SATURATE = 448.0
EPSILON = 1e-06
ROPE_BASE = 1000000.0
MASKED_SCORE = -1e30


def partner(value, axis, bit):
    mask = 2**bit
    pairs = [(source, source ^ mask) for source in range(lax.axis_size(axis))]
    return lax.ppermute(value, axis, pairs)


def quantize(weight, scale):
    scaled = weight.astype(jnp.float32) / scale
    return jnp.clip(scaled, -SATURATE, SATURATE).astype(jnp.bfloat16)


def documents(lengths, window):
    doc_ends = jnp.cumsum(lengths)
    doc_starts = doc_ends - lengths
    places = jnp.arange(window, dtype=jnp.int32)
    doc_ids = jnp.sum((places[:, None] >= doc_ends[None, :]).astype(jnp.int32), axis=1)
    labels = jnp.arange(lengths.shape[0], dtype=jnp.int32)
    doc_begin = jnp.sum(
        jnp.where(doc_ids[:, None] == labels[None, :], doc_starts[None, :], 0), axis=1
    )
    return (doc_ids, places - doc_begin)


def rope_tables(position, head_dim):
    half_dim = head_dim // 2
    frequency = jnp.exp(
        jnp.arange(half_dim, dtype=jnp.float32) * (-2.0 * math.log(ROPE_BASE) / head_dim)
    )
    angles = position.astype(jnp.float32)[:, None] * frequency[None, :]
    return (jnp.cos(angles), jnp.sin(angles))


def rotate(vectors, cosine_table, sine_table):
    half_dim = vectors.shape[-1] // 2
    front_half = vectors[..., :half_dim]
    back_half = vectors[..., half_dim:]
    cos_part = cosine_table[:, None, :]
    sin_part = sine_table[:, None, :]
    return jnp.concatenate(
        [
            front_half * cos_part - back_half * sin_part,
            back_half * cos_part + front_half * sin_part,
        ],
        axis=-1,
    )


def join_pair(own_piece, other_piece, upper_bit):
    low_half = jnp.where(upper_bit == 1, other_piece, own_piece)
    high_half = jnp.where(upper_bit == 1, own_piece, other_piece)
    return jnp.concatenate([low_half, high_half], axis=-1)


def pair_weights(key_part, value_part, tp_index):
    other_key, other_value = partner((key_part, value_part), "tp", 0)
    upper_bit = tp_index // 2**0 % 2
    key_part = join_pair(key_part, other_key, upper_bit)
    value_part = join_pair(value_part, other_value, upper_bit)
    return (key_part, value_part)


def reorder_rows(row_major, tp_count, fsdp_count):
    width = row_major.shape[1]
    return (
        row_major.reshape(tp_count, fsdp_count, -1, width).transpose(1, 0, 2, 3).reshape(-1, width)
    )


def reorder_cols(col_major, tp_count, fsdp_count):
    height = col_major.shape[0]
    return (
        col_major.reshape(height, tp_count, fsdp_count, -1)
        .transpose(0, 2, 1, 3)
        .reshape(height, -1)
    )


def shards(
    hidden_in,
    lengths,
    norm_gain,
    query_weight,
    key_weight,
    value_weight,
    out_weight,
    query_scale,
    key_scale,
    value_scale,
    out_scale,
):
    tp_count = lax.axis_size("tp")
    fsdp_count = lax.axis_size("fsdp")
    tp_index = lax.axis_index("tp")
    fsdp_index = lax.axis_index("fsdp")
    tokens = hidden_in.shape[0]
    share_count = tp_count // KV
    q_width = query_weight.shape[1] // tp_count
    block_cols = out_weight.shape[1]
    query_cast = quantize(query_weight, query_scale)
    key_cast = quantize(key_weight, key_scale)
    value_cast = quantize(value_weight, value_scale)
    flat_index = fsdp_index * tp_count + tp_index
    out_cast = quantize(
        out_weight, lax.dynamic_slice_in_dim(out_scale, flat_index * block_cols, block_cols)
    )
    widened = hidden_in.astype(jnp.float32)
    inv_rms = lax.rsqrt(jnp.mean(widened * widened, axis=1, keepdims=True) + EPSILON)
    normed = (widened * inv_rms * norm_gain).astype(jnp.bfloat16)
    doc_ids, position = documents(lengths[0], tokens)
    cosine_table, sine_table = rope_tables(position, HD)
    query_rows, key_rows, value_rows = (
        lax.all_gather(query_cast, "fsdp", axis=0, tiled=True),
        lax.all_gather(key_cast, "fsdp", axis=0, tiled=True),
        lax.all_gather(value_cast, "fsdp", axis=0, tiled=True),
    )
    query_full, key_full, value_full = (
        lax.all_to_all(query_rows, "tp", split_axis=1, concat_axis=0, tiled=True),
        lax.all_to_all(key_rows, "tp", split_axis=1, concat_axis=0, tiled=True),
        lax.all_to_all(value_rows, "tp", split_axis=1, concat_axis=0, tiled=True),
    )
    query_full = reorder_rows(query_full, tp_count, fsdp_count)
    key_full = reorder_rows(key_full, tp_count, fsdp_count)
    value_full = reorder_rows(value_full, tp_count, fsdp_count)
    key_full, value_full = pair_weights(key_full, value_full, tp_index)
    query_proj = jnp.dot(normed, query_full, preferred_element_type=jnp.float32)
    key_proj = jnp.dot(normed, key_full, preferred_element_type=jnp.float32)
    value_proj = jnp.dot(normed, value_full, preferred_element_type=jnp.float32)
    out_cols = lax.all_gather(out_cast, "fsdp", axis=1, tiled=True)
    out_local = lax.all_to_all(out_cols, "tp", split_axis=0, concat_axis=1, tiled=True)
    out_local = reorder_cols(out_local, tp_count, fsdp_count)
    query_cols = lax.dynamic_slice_in_dim(query_scale, tp_index * q_width, q_width)
    queries = rotate(
        (query_proj * query_cols).reshape(tokens, q_width // HD, HD), cosine_table, sine_table
    ).astype(jnp.bfloat16)
    head_start = tp_index // share_count * HD
    key_raw = (key_proj * lax.dynamic_slice_in_dim(key_scale, head_start, HD)).astype(jnp.bfloat16)
    values = (value_proj * lax.dynamic_slice_in_dim(value_scale, head_start, HD)).astype(
        jnp.bfloat16
    )
    key_raw = lax.optimization_barrier(key_raw)
    key_rot = rotate(
        key_raw.astype(jnp.float32).reshape(tokens, 1, HD), cosine_table, sine_table
    ).astype(jnp.bfloat16)
    key_rot = key_rot.reshape(tokens, HD)
    places = jnp.arange(tokens, dtype=jnp.int32)
    allowed = (doc_ids[:, None] == doc_ids[None, :]) & (places[None, :] <= places[:, None])
    scores = jnp.einsum(
        "thd,sd->hts", queries, key_rot, preferred_element_type=jnp.float32
    ) * HD ** (-0.5)
    scores = jnp.where(allowed[None, :, :], scores, MASKED_SCORE)
    row_max = jnp.max(scores, axis=2, keepdims=True)
    weights = jnp.exp(scores - row_max)
    probabilities = (weights / jnp.sum(weights, axis=2, keepdims=True)).astype(jnp.bfloat16)
    attended = jnp.einsum(
        "hts,sd->thd", probabilities, values, preferred_element_type=jnp.float32
    ).astype(jnp.bfloat16)
    attended = attended.reshape(tokens, q_width)
    summed = lax.psum_scatter(
        jnp.dot(attended, out_local, preferred_element_type=jnp.float32).astype(jnp.bfloat16),
        "tp",
        scatter_dimension=0,
        tiled=True,
    ).astype(jnp.float32)
    return (summed * out_scale).astype(jnp.bfloat16)


def solution(mesh):
    in_specs = (
        P("fsdp", None),
        P("fsdp", None),
        P(),
        P(("fsdp", "tp"), None),
        P(("fsdp", "tp"), None),
        P(("fsdp", "tp"), None),
        P(None, ("fsdp", "tp")),
        P(),
        P(),
        P(),
        P(),
    )
    out_specs = P(("fsdp", "tp"), None)
    return jax.shard_map(shards, mesh=mesh, in_specs=in_specs, out_specs=out_specs, check_vma=False)
```

profile of v0, /device:TPU:1, one launch (start us, length us, event | category | flops | bytes accessed | tf_op | source)
XLA Modules:
  0.0 715.9 jit_solution(9141102185887608385)
XLA Ops:
  10.0 2.5 clamp_convert_fusion.1
  14.6 44.8 %all-gather.7.cloned.1.call-done = bf16[512,1024]{1,0:T(8,128)(2,1)} async-done(((bf16[64,1024]{1,0:T(8,128)(2,1)}), bf16[512,1024]{1,0:T(8,128)(2,1)}) %all-gather.7.cloned.1.call-update) | async-done | bytes 1048592 | tf_op jit(solution)/shard_map/all_gather | solution.py:130
  59.4 2.3 copy.62
  61.7 6.0 all-to-all-start.1
  67.7 47.0 %all-gather.5.cloned.1.call-done = bf16[512,1024]{1,0:T(8,128)(2,1)} async-done(((bf16[64,1024]{1,0:T(8,128)(2,1)}), bf16[512,1024]{1,0:T(8,128)(2,1)}) %all-gather.5.cloned.1.call-update) | async-done | bytes 1048592 | tf_op jit(solution)/shard_map/all_gather | solution.py:131
  114.7 2.3 copy.60
  117.0 6.0 all-to-all-start
  123.0 108.6 %all-gather.9.cloned.1.call-done = bf16[512,8192]{1,0:T(8,128)(2,1)} async-done(((bf16[64,8192]{1,0:T(8,128)(2,1)}), bf16[512,8192]{1,0:T(8,128)(2,1)}) %all-gather.9.cloned.1.call-update) | async-done | bytes 8388624 | tf_op jit(solution)/shard_map/all_gather | solution.py:129
  231.6 11.5 %copy.64 = bf16[512,8192]{0,1:T(8,128)(2,1)} copy(bf16[512,8192]{1,0:T(8,128)(2,1)} %all-gather.9.cloned.1.call-done) | data formatting | bytes 16777216 | tf_op jit(solution)/shard_map/all_gather | solution.py:129
  244.1 5.6 all-to-all-start.2
  249.7 167.2 %all-gather.11.cloned.1.call-done = bf16[8192,512]{0,1:T(8,128)(2,1)} async-done(((bf16[8192,64]{0,1:T(8,128)(2,1)}), bf16[8192,512]{0,1:T(8,128)(2,1)}) %all-gather.11.cloned.1.call-update) | async-done | bytes 8388624 | tf_op jit(solution)/shard_map/all_gather | solution.py:145
  416.9 12.0 %copy.71 = bf16[8192,512]{1,0:T(8,128)(2,1)} copy(bf16[8192,512]{0,1:T(8,128)(2,1)} %all-gather.11.cloned.1.call-done) | data formatting | bytes 16777216 | tf_op jit(solution)/shard_map/all_gather | solution.py:145
  428.9 5.7 all-to-all-start.3
  435.0 5.1 fusion.1
  441.2 3.8 copy.81
  445.0 3.3 reshape.244
  448.9 2.8 reshape.240
  451.6 3.8 copy.82
  455.4 3.3 reshape.241
  464.1 2.8 broadcast_select_fusion.1
  467.0 5.8 fusion.27
  474.0 12.3 %copy.65 = bf16[16,512,512]{2,1,0:T(8,128)(2,1)} copy(bf16[16,512,512]{1,2,0:T(8,128)(2,1)} %bitcast.17) | data formatting | bytes 16777216 | tf_op jit(solution)/shard_map/all_to_all | solution.py:134
  486.3 7.7 %copy.66 = bf16[8,16,64,512]{3,2,1,0:T(8,128)(2,1)} copy(bf16[8,16,64,512]{3,2,0,1:T(8,128)(2,1)} %bitcast.84) | data formatting | bytes 16777216 | tf_op jit(solution)/shard_map/transpose | solution.py:82
  494.1 12.8 %convolution_multiply_fusion = f32[512,512]{0,1:T(8,128)S(1)} fusion(bf16[8192,512]{1,0:T(8,128)(2,1)} %bitcast.87, f32[512]{0:T(512)S(1)} %dynamic_slice.14, bf16[512,8192]{1,0:T(8,128)(2,1)} %param.11, f32[8192]{0:T(1024)S(1)} %copy-done.8, f32[512]{0:T(512)S(1)} %add_rsqrt_fusion), kind=kOutput, calls=%fused_computation.27 | convolution fusion | flops 4312006656 | bytes 17862656 | tf_op jit(solution)/shard_map/dot_general | solution.py:142
  507.7 56.3 %all-to-all-done.3 = bf16[16,512,512]{2,1,0:T(8,128)(2,1)} async-done(((bf16[16,512,512]{2,1,0:T(8,128)(2,1)}), bf16[16,512,512]{2,1,0:T(8,128)(2,1)}, u32[]{:S(2)}, u32[]{:S(2)}) %all-to-all-start.3) | async-done | bytes 8388640 | tf_op jit(solution)/shard_map/all_to_all | solution.py:146
  564.0 12.3 %copy.72 = bf16[512,16,512]{0,2,1:T(8,128)(2,1)} copy(bf16[512,16,512]{2,0,1:T(8,128)(2,1)} %bitcast.26) | data formatting | bytes 16777216 | tf_op jit(solution)/shard_map/all_to_all | solution.py:146
  576.3 7.8 %copy.73 = bf16[512,8,16,64]{0,3,2,1:T(8,128)(2,1)} copy(bf16[512,8,16,64]{0,3,1,2:T(8,128)(2,1)} %bitcast.85) | data formatting | bytes 16777216 | tf_op jit(solution)/shard_map/transpose | solution.py:90
  585.2 1.8 fusion.65
  588.3 10.3 %fusion.17 = bf16[128,4,512]{2,0,1:T(8,128)(2,1)S(1)} fusion(f32[4,512]{1,0:T(4,128)S(1)} %fusion.65, bf16[8192,64]{0,1:T(8,128)(2,1)S(1)} %copy-done.3, bf16[8192,64]{0,1:T(8,128)(2,1)S(1)} %copy-done.4, f32[128]{0:T(128)S(1)} %dynamic_slice.12, bf16[512,8192]{1,0:T(8,128)(2,1)} %param.11, f32[8192]{0:T(1024)S(1)} %copy-done.8, f32[512]{0:T(512)S(1)} %add_rsqrt_fusion, ...), kind=kOutput, calls=%fused_computation.28 | convolution fusion | flops 1370884608 | bytes 15510016 | tf_op jit(solution)/shard_map/hts,sd->thd/dot_general | solution.py:171
  598.6 10.2 %convolution_convert_fusion = bf16[512,8192]{1,0:T(8,128)(2,1)} fusion(bf16[512,512]{0,1:T(8,128)(2,1)S(1)} %bitcast.95, bf16[512,8192]{0,1:T(8,128)(2,1)} %bitcast.86), kind=kOutput, calls=%fused_computation.6 | convolution fusion | flops 4299161600 | bytes 17301504 | tf_op jit(solution)/shard_map/dot_general | solution.py:176
  608.8 98.6 %reduce-scatter.2.cloned.1.call-done = bf16[32,8192]{1,0:T(8,128)(2,1)} async-done(((bf16[512,8192]{1,0:T(8,128)(2,1)}), bf16[32,8192]{1,0:T(8,128)(2,1)}) %reduce-scatter.2.cloned.1.call-update) | async-done | bytes 524304 | tf_op jit(solution)/shard_map/reduce_scatter | solution.py:175
  707.5 1.9 multiply_convert_fusion
  (61 shorter events, 18.3 us)
Async XLA Ops:
  6.5 6.7 copy-start.5
  6.5 52.9 %all-gather.7.cloned.1.call-start = ((), (), s32[]{:S(2)}) async-start(), calls=%async_computation.6 | async-start | bytes 1179648 | tf_op jit(solution)/shard_map/all_gather | solution.py:130
  8.2 106.5 %all-gather.5.cloned.1.call-start = ((), (), s32[]{:S(2)}) async-start(), calls=%async_computation.5 | async-start | bytes 1179648 | tf_op jit(solution)/shard_map/all_gather | solution.py:131
  9.9 221.7 %all-gather.9.cloned.1.call-start = ((), (), s32[]{:S(2)}) async-start(), calls=%async_computation.7 | async-start | bytes 9437184 | tf_op jit(solution)/shard_map/all_gather | solution.py:129
  12.4 404.5 %all-gather.11.cloned.1.call-start = ((), (), s32[]{:S(2)}) async-start(), calls=%async_computation.8 | async-start | bytes 9437184 | tf_op jit(solution)/shard_map/all_gather | solution.py:145
  61.7 55.3 %all-to-all-start.1 = ((bf16[512,16,64]{0,2,1:T(8,128)(2,1)}), bf16[512,16,64]{0,2,1:T(8,128)(2,1)S(1)}, u32[]{:S(2)}, u32[]{:S(2)}) async-start(bf16[512,16,64]{0,2,1:T(8,128)(2,1)} %bitcast.6), calls=%async_computation.1 | async-start | bytes 2097152 | tf_op jit(solution)/shard_map/all_to_all | solution.py:135
  117.0 126.1 %all-to-all-start = ((bf16[512,16,64]{0,2,1:T(8,128)(2,1)}), bf16[512,16,64]{0,2,1:T(8,128)(2,1)S(1)}, u32[]{:S(2)}, u32[]{:S(2)}) async-start(bf16[512,16,64]{0,2,1:T(8,128)(2,1)} %bitcast), calls=%async_computation | async-start | bytes 2097152 | tf_op jit(solution)/shard_map/all_to_all | solution.py:136
  243.1 1.0 copy-start
  244.1 184.8 %all-to-all-start.2 = ((bf16[512,16,512]{0,2,1:T(8,128)(2,1)}), bf16[512,16,512]{0,2,1:T(8,128)(2,1)}, u32[]{:S(2)}, u32[]{:S(2)}) async-start(bf16[512,16,512]{0,2,1:T(8,128)(2,1)} %bitcast.83), calls=%async_computation.2 | async-start | bytes 16777216 | tf_op jit(solution)/shard_map/all_to_all | solution.py:134
  428.9 5.8 copy-start.9
  428.9 135.0 %all-to-all-start.3 = ((bf16[16,512,512]{2,1,0:T(8,128)(2,1)}), bf16[16,512,512]{2,1,0:T(8,128)(2,1)}, u32[]{:S(2)}, u32[]{:S(2)}) async-start(bf16[16,512,512]{2,1,0:T(8,128)(2,1)} %bitcast.82), calls=%async_computation.3 | async-start | bytes 16777216 | tf_op jit(solution)/shard_map/all_to_all | solution.py:146
  434.7 272.8 %reduce-scatter.2.cloned.1.call-start = ((), (), s32[]{:S(2)}) async-start(), calls=%async_computation.9 | async-start | bytes 8912896 | tf_op jit(solution)/shard_map/reduce_scatter | solution.py:175
  448.3 15.8 %collective-permute-start.1 = (bf16[8192,64]{0,1:T(8,128)(2,1)S(1)}, bf16[8192,64]{0,1:T(8,128)(2,1)}, u32[]{:S(2)}, u32[]{:S(2)}) collective-permute-start(bf16[8192,64]{0,1:T(8,128)(2,1)S(1)} %reshape.244), channel_id=1, source_target_pairs={{0,1},{1,0},{2,3},{3,2},{4,5},{5,4},{6,7},{7,6},{8,9},{9,8},{10,11... | collective-permute-start | bytes 3145736 | tf_op jit(solution)/shard_map/ppermute | solution.py:21
  458.8 5.4 collective-permute-start
  464.1 2.8 copy-start.8
  576.3 7.8 %copy-start.2 = (f32[512,64]{1,0:T(8,128)S(1)}, f32[512,64]{1,0:T(8,128)}, u32[]{:S(2)}) copy-start(f32[512,64]{1,0:T(8,128)} %get-tuple-element.16) | copy-start | bytes 393220
  584.1 1.1 copy-start.6
  585.2 2.1 copy-start.1
  585.2 2.1 copy-start.3
  585.2 3.0 copy-start.4
  608.8 98.7 %copy-start.7 = (f32[8192]{0:T(1024)S(1)}, f32[8192]{0:T(1024)}, u32[]{:S(2)}) copy-start(f32[8192]{0:T(1024)} %param.21) | copy-start | bytes 98308
Sparse Core Ops, SparseCore 0:
  9.7 49.6 all-gather.6
  61.8 52.9 all-gather.4
  117.0 114.5 all-gather.8
  233.8 183.0 all-gather.10
  609.0 98.4 reduce-scatter.1
where the time goes:
time: 718 us; the launch traced here: 716 us
  waiting for transfers between devices  523 us (73%)
  local copies, waits for them, and re-layouts  92.5 us (13%)
  matrix products  40 us (6%)
  starting transfers between devices  24.2 us (3%)
  other arithmetic  23.2 us (3%)
  between operations  13.3 us (2%)
    all_gather x1, waiting for transfers between devices, shards(): out_cols = lax.all_gather(out_cast, 'fsdp', axis=1, tiled=True)  167 us
    all_gather x1, waiting for transfers between devices, shards(): lax.all_gather(query_cast, 'fsdp', axis=0, tiled=True)  109 us
    reduce_scatter x1, waiting for transfers between devices, shards(): lax.psum_scatter(jnp.dot(attended, out_local, preferred_element_type=jnp....  98.6 us
    all_to_all x1, waiting for transfers between devices, shards(): lax.all_to_all(out_cols, 'tp', split_axis=0, concat_axis=1, tiled=True)  56.3 us
    all_gather x1, waiting for transfers between devices, shards(): lax.all_gather(value_cast, 'fsdp', axis=0, tiled=True)  47 us
    all_gather x1, waiting for transfers between devices, shards(): lax.all_gather(key_cast, 'fsdp', axis=0, tiled=True)  44.8 us
    reshape x6, local copies, waits for them, and re-layouts, reorder_rows(): row_major.reshape(tp_count, fsdp_count, -1, width).transpose(1, 0, 2, 3)  18.1 us
  transfers between devices with their start and end apart: 11, of which 6 were waited for; matrix products, arithmetic and copies ran while one was open for 15% of the time, Pallas kernels for 0%

commit v1 on v0

v1 whole, which is shorter than its diff:
```python
import math

import jax
import jax.numpy as jnp
from jax import lax
from jax.experimental import pallas as pl
from jax.experimental.pallas import tpu as pltpu
from jax.sharding import PartitionSpec as P

MESH = pl.DeviceIdType.MESH
F32 = jnp.float32
BF16 = jnp.bfloat16

HD = 128
TOK = 512
D = 8192
SATURATE = 448.0
EPSILON = 1e-06
ROPE_BASE = 1000000.0
MASKED_SCORE = -1e30

TREE = {
    (1, 0): (0, 0, 1),
    (3, 0): (0, 0, -1),
    (0, 1): (0, 0, 0),
    (2, 0): (1, 0, 1),
    (2, 1): (2, 0, 0),
    (1, 1): (0, 1, 1),
    (3, 1): (0, 1, -1),
}


class Gather:
    def __init__(self, slot, piece, send_sem, recv_sem, plus, minus, pair):
        self.slot, self.piece = slot, piece
        self.send_sem, self.recv_sem = send_sem, recv_sem
        self.to = {1: plus, -1: minus, 0: pair}

    def index(self, u, dz, h):
        return self.slot(u if h == 0 else (4 - u) % 4, dz)

    def copy(self, u, dz, h):
        su, sdz, step = TREE[(u, dz)]
        ref = self.piece(self.index(su, sdz, h), h)
        return pltpu.make_async_remote_copy(
            src_ref=ref,
            dst_ref=ref,
            send_sem=self.send_sem.at[h, u * 2 + dz],
            recv_sem=self.recv_sem.at[h, u * 2 + dz],
            device_id=self.to[step if h == 0 else -step],
            device_id_type=MESH,
        )

    def send(self, h, *targets):
        for u, dz in targets:
            self.copy(u, dz, h).start()

    def arrived(self, u, dz, h):
        ref = self.piece(self.index(u, dz, h), h)
        pltpu.make_async_remote_copy(
            src_ref=ref,
            dst_ref=ref,
            send_sem=self.send_sem.at[h, u * 2 + dz],
            recv_sem=self.recv_sem.at[h, u * 2 + dz],
            device_id=self.to[0],
            device_id_type=MESH,
        ).wait_recv()

    def sent(self):
        for h in range(2):
            for u, dz in TREE:
                self.copy(u, dz, h).wait_send()


def choose(i, values):
    result = values[-1]
    for n in range(len(values) - 2, -1, -1):
        result = jnp.where(i == n, values[n], result)
    return result


def kernel(
    hidden_ref, lengths_ref, gain_ref, wq_ref, wk_ref, wv_ref, wo_ref, qs_ref, ks_ref, vs_ref, os_ref,
    out_ref,
    nrm, raw_q, raw_k, raw_v, raw_o, snd, wqkv, wo, ww_own, ww_snd, ww_got, acc, cos_t, sin_t, begin_t,
    q_t, kv_t, att, acc_o, ost, got,
    load_sem, a2a_s, a2a_r, core_s, core_r, q_s, q_r, o_s, o_r, att_s, att_r, fin_s, fin_r,
):
    f = lax.axis_index("fsdp")
    t = lax.axis_index("tp")
    x, zh = f // 2, f % 2
    y, zl, c = t // 4, (t // 2) % 2, t % 2
    rz = (zl + zh) % 2
    role = y * 2 + rz
    hb = role * 2 + c

    def device(ff, tt):
        return {"fsdp": ff, "tp": tt}

    x_plus = device(((x + 1) % 4) * 2 + zh, t)
    x_minus = device(((x + 3) % 4) * 2 + zh, t)
    z_pair = device(x * 2 + 1 - zh, y * 4 + (1 - zl) * 2 + c)
    y_plus = device(f, ((y + 1) % 4) * 4 + zl * 2 + c)
    y_minus = device(f, ((y + 3) % 4) * 4 + zl * 2 + c)
    zl_pair = device(f, y * 4 + (1 - zl) * 2 + c)
    core_pair = device(f, y * 4 + zl * 2 + 1 - c)

    barrier = pltpu.get_barrier_semaphore()
    for other in (x_plus, x_minus, z_pair):
        pl.semaphore_signal(barrier, inc=1, device_id=other, device_id_type=MESH)

    @pl.loop(1, 16)
    def _(i):
        pl.semaphore_signal(barrier, inc=1, device_id=device(f, (t + i) % 16), device_id_type=MESH)

    loads = [
        pltpu.make_async_copy(src, dst, load_sem.at[n])
        for n, (src, dst) in enumerate(
            [(wq_ref, raw_q), (wk_ref, raw_k), (wv_ref, raw_v), (wo_ref, raw_o), (hidden_ref, nrm)]
        )
    ]
    for load in loads:
        load.start()

    def quantize(weight, inverse):
        return jnp.clip(weight.astype(F32) * inverse, -SATURATE, SATURATE).astype(BF16)

    for load in loads[:3]:
        load.wait()

    @pl.loop(0, 8)
    def _(r):
        for n in range(2):
            cols = pl.ds(pl.multiple_of((r * 2 + n) * 512, 512), 512)
            snd[r * 2 + n, :, 0:512] = quantize(raw_q[:, cols], 1.0 / qs_ref[:, cols])
        cols = pl.ds(pl.multiple_of(r * 128, 128), 128)
        snd[r * 2, :, 512:640] = quantize(raw_k[:, cols], 1.0 / ks_ref[:, cols])
        snd[r * 2 + 1, :, 512:640] = quantize(raw_v[:, cols], 1.0 / vs_ref[:, cols])

    pl.semaphore_wait(barrier, 18)

    def block_copy(i):
        to = (t + i) % 16
        block = ((to // 4) * 2 + ((to // 2) % 2 + zh) % 2) * 2 + to % 2
        return pltpu.make_async_remote_copy(
            src_ref=snd.at[block],
            dst_ref=wqkv.at[f, pl.ds(pl.multiple_of(t * 64, 64), 64)],
            send_sem=a2a_s.at[i],
            recv_sem=a2a_r.at[i],
            device_id=device(f, to),
            device_id_type=MESH,
        )

    @pl.loop(1, 16)
    def _(i):
        block_copy(i).start()

    wqkv[f, pl.ds(pl.multiple_of(t * 64, 64), 64)] = snd[hb]

    loads[3].wait()
    chip_cols = pl.ds(pl.multiple_of((f * 8 + t // 2) * 128, 128), 128)
    chip_scale = 1.0 / os_ref[:, chip_cols]
    own_scale = jnp.where(c == 0, chip_scale[:, :64], chip_scale[:, 64:])

    def twice(block):
        part = quantize(raw_o[pl.ds(pl.multiple_of(block * 512, 512), 512), :], own_scale)
        return jnp.concatenate([part, part], axis=1)

    @pl.loop(0, 8)
    def _(r):
        ww_snd[pl.ds(pl.multiple_of(r * 512, 512), 512)] = twice(r * 2 + 1 - c)

    core_w = pltpu.make_async_remote_copy(
        src_ref=ww_snd, dst_ref=ww_got, send_sem=core_s.at[0], recv_sem=core_r.at[0],
        device_id=core_pair, device_id_type=MESH,
    )
    core_w.start()

    @pl.loop(0, 8)
    def _(r):
        ww_own[pl.ds(pl.multiple_of(r * 512, 512), 512)] = twice(r * 2 + c)

    core_w.wait_recv()

    @pl.loop(0, 8)
    def _(r):
        rows = pl.ds(pl.multiple_of(r * 512, 512), 512)
        lane = lax.broadcasted_iota(jnp.int32, (512, 128), 1)
        mine = (lane // 64) == c
        wo[f, rows] = jnp.where(mine, ww_own[rows].astype(F32), ww_got[rows].astype(F32)).astype(BF16)

    def fsdp_slot(dx, dz):
        return ((x + 4 - dx) % 4) * 2 + (zh + dz) % 2

    out_gather = Gather(
        fsdp_slot, lambda s, h: wo.at[s, pl.ds(h * 2048, 2048)], o_s, o_r, x_plus, x_minus, z_pair
    )
    in_gather = Gather(
        fsdp_slot, lambda s, h: wqkv.at[s, pl.ds(h * 512, 512)], q_s, q_r, x_plus, x_minus, z_pair
    )
    att_gather = Gather(
        lambda dy, dz: ((y + 4 - dy) % 4) * 2 + (rz + dz) % 2,
        lambda s, h: att.at[s, h], att_s, att_r, y_plus, y_minus, zl_pair,
    )
    for h in range(2):
        out_gather.send(h, (1, 0), (3, 0), (0, 1))

    loads[4].wait()

    @pl.loop(0, 32)
    def _(i):
        rows = pl.ds(pl.multiple_of(i * 16, 16), 16)
        wide = nrm[rows, :].astype(F32)
        inverse = lax.rsqrt(jnp.mean(wide * wide, axis=1, keepdims=True) + EPSILON)
        nrm[rows, :] = (wide * inverse * gain_ref[...]).astype(BF16)

    place = lax.broadcasted_iota(jnp.int32, (TOK, 128), 0)
    begin = jnp.zeros((TOK, 128), jnp.int32)
    start = lengths_ref[0, 0]
    for n in range(1, 8):
        begin = jnp.where(place >= start, start, begin)
        start = start + lengths_ref[0, n]
    begin_t[...] = begin
    lane = lax.broadcasted_iota(jnp.int32, (TOK, 128), 1)
    frequency = jnp.exp((lane % 64).astype(F32) * (-2.0 * math.log(ROPE_BASE) / HD))
    angle = (place - begin).astype(F32) * frequency
    cos_t[...] = jnp.cos(angle)
    sine = jnp.sin(angle)
    sin_t[...] = jnp.where(lane < 64, -sine, sine)

    for h in range(2):
        @pl.loop(h * 8, h * 8 + 8)
        def _(src):
            @pl.when(src != t)
            def _():
                ref = wqkv.at[f, pl.ds(pl.multiple_of(src * 64, 64), 64)]
                i = (t + 16 - src) % 16
                pltpu.make_async_remote_copy(
                    src_ref=ref, dst_ref=ref, send_sem=a2a_s.at[i], recv_sem=a2a_r.at[i],
                    device_id=core_pair, device_id_type=MESH,
                ).wait_recv()

        in_gather.send(h, (1, 0), (3, 0), (0, 1))

    acc[...] = jnp.zeros_like(acc)

    def project(*pieces):
        slots = [in_gather.index(u, dz, h) for u, dz, h in pieces]
        halves = [h for _, _, h in pieces]

        @pl.loop(0, len(pieces))
        def _(i):
            s, h = choose(i, slots), choose(i, halves)
            cols = pl.ds(pl.multiple_of(s * 1024 + h * 512, 512), 512)
            acc[...] += jnp.dot(
                nrm[:, cols], wqkv[s, pl.ds(pl.multiple_of(h * 512, 512), 512), :], preferred_element_type=F32
            )

    project((0, 0, 0), (0, 0, 1))
    for h in range(2):
        in_gather.arrived(1, 0, h)
        in_gather.send(h, (2, 0))
    in_gather.arrived(0, 1, 0)
    in_gather.send(0, (1, 1), (3, 1))
    project((1, 0, 0), (1, 0, 1), (0, 1, 0))
    for h in range(2):
        in_gather.arrived(3, 0, h)
    in_gather.arrived(0, 1, 1)
    in_gather.send(1, (1, 1), (3, 1))
    project((3, 0, 0), (3, 0, 1), (0, 1, 1))
    for h in range(2):
        in_gather.arrived(2, 0, h)
        in_gather.send(h, (2, 1))
    project((2, 0, 0), (2, 0, 1))
    in_gather.arrived(1, 1, 0)
    in_gather.arrived(1, 1, 1)
    for h in range(2):
        out_gather.arrived(1, 0, h)
        out_gather.send(h, (2, 0))
    in_gather.arrived(2, 1, 0)
    project((1, 1, 0), (1, 1, 1), (2, 1, 0))
    in_gather.arrived(3, 1, 0)
    in_gather.arrived(3, 1, 1)
    for h in range(2):
        out_gather.arrived(0, 1, h)
        out_gather.send(h, (1, 1), (3, 1))
    in_gather.arrived(2, 1, 1)
    project((3, 1, 0), (3, 1, 1), (2, 1, 1))

    def rope(v):
        return v * cos_t[...] + pltpu.roll(v, 64, axis=1) * sin_t[...]

    kv_cols = pl.ds(pl.multiple_of(role * 128, 128), 128)
    key_raw = (acc[:, 512:640] * ks_ref[:, kv_cols]).astype(BF16).astype(F32)
    value = acc[:, 512:640] * vs_ref[:, kv_cols]
    kv_t[c] = jnp.where(c == 0, rope(key_raw), value).astype(BF16)
    core_kv = pltpu.make_async_remote_copy(
        src_ref=kv_t.at[c], dst_ref=kv_t.at[c], send_sem=core_s.at[1], recv_sem=core_r.at[1],
        device_id=core_pair, device_id_type=MESH,
    )
    core_kv.start()

    @pl.loop(0, 4)
    def _(n):
        cols = pl.ds(pl.multiple_of(n * 128, 128), 128)
        scale = qs_ref[:, pl.ds(pl.multiple_of(hb * 512 + n * 128, 128), 128)]
        q_t[n] = rope(acc[:, cols] * scale).astype(BF16)

    other = kv_t.at[1 - c]
    pltpu.make_async_remote_copy(
        src_ref=other, dst_ref=other, send_sem=core_s.at[1], recv_sem=core_r.at[1],
        device_id=core_pair, device_id_type=MESH,
    ).wait_recv()

    for h in range(2):
        for n in range(2):
            for b in range(4):
                first = max(0, b * 128 - 256)
                width = (b + 1) * 128 - first
                rows = slice(b * 128, (b + 1) * 128)
                keys = slice(first, first + width)
                scores = lax.dot_general(
                    q_t[h * 2 + n, rows], kv_t[0, keys], (((1,), (1,)), ((), ())), preferred_element_type=F32
                ) * HD ** (-0.5)
                p = lax.broadcasted_iota(jnp.int32, (128, width), 0) + b * 128
                s = lax.broadcasted_iota(jnp.int32, (128, width), 1) + first
                keep = (s <= p) & (s >= begin_t[rows, 0:1])
                scores = jnp.where(keep, scores, MASKED_SCORE)
                weights = jnp.exp(scores - jnp.max(scores, axis=1, keepdims=True))
                total = jnp.sum(weights, axis=1, keepdims=True)
                mixed = jnp.dot(weights.astype(BF16), kv_t[1, keys], preferred_element_type=F32)
                att[role, h, rows, n * 128:(n + 1) * 128] = (mixed / total).astype(BF16)
        att_gather.send(h, (1, 0), (3, 0), (0, 1))

    early = [fsdp_slot(dx, dz) for dx, dz in ((0, 0), (1, 0), (3, 0), (0, 1))]
    late = [fsdp_slot(dx, dz) for dx, dz in ((2, 0), (1, 1), (3, 1), (2, 1))]

    def mix(which, slots, pieces):
        roles = [att_gather.index(u, dz, h) for u, dz, h in pieces]
        halves = [h for _, _, h in pieces]

        @pl.loop(0, len(pieces))
        def _(i):
            r, h = choose(i, roles), choose(i, halves)
            rows = pl.ds(pl.multiple_of(r * 512 + h * 256, 256), 256)
            columns = jnp.concatenate([wo[s, rows] for s in slots], axis=1)
            acc_o[which] += jnp.dot(att[r, h], columns, preferred_element_type=F32)

    def finish(which):
        ost[which] = acc_o[which].astype(BF16)

        @pl.loop(1, 16)
        def _(i):
            final_copy(which, i).start()

        got[which, t] = ost[which, pl.ds(pl.multiple_of(t * 32, 32), 32)]

    def final_copy(which, i):
        to = (t + i) % 16
        return pltpu.make_async_remote_copy(
            src_ref=ost.at[which, pl.ds(pl.multiple_of(to * 32, 32), 32)],
            dst_ref=got.at[which, t],
            send_sem=fin_s.at[which, i],
            recv_sem=fin_r.at[which, i],
            device_id=device(f, to),
            device_id_type=MESH,
        )

    acc_o[...] = jnp.zeros_like(acc_o)
    for h in range(2):
        out_gather.arrived(3, 0, h)
    mix(0, early, [(0, 0, 0), (0, 0, 1)])
    for h in range(2):
        att_gather.arrived(1, 0, h)
        att_gather.send(h, (2, 0))
        att_gather.arrived(0, 1, h)
        att_gather.send(h, (1, 1), (3, 1))
    mix(0, early, [(1, 0, 0), (1, 0, 1), (0, 1, 0), (0, 1, 1)])
    for h in range(2):
        out_gather.arrived(2, 0, h)
        out_gather.send(h, (2, 1))
    for h in range(2):
        att_gather.arrived(3, 0, h)
    for h in range(2):
        att_gather.arrived(2, 0, h)
        att_gather.send(h, (2, 1))
    mix(0, early, [(3, 0, 0), (3, 0, 1), (2, 0, 0), (2, 0, 1)])
    for h in range(2):
        for u in (1, 3, 2):
            att_gather.arrived(u, 1, h)
    mix(0, early, [(u, 1, h) for u in (1, 3, 2) for h in range(2)])
    finish(0)
    for h in range(2):
        for u in (1, 3, 2):
            out_gather.arrived(u, 1, h)
    mix(1, late, [(u, dz, h) for u in range(4) for dz in range(2) for h in range(2)])
    finish(1)

    def collect(which, offsets):
        @pl.loop(1, 16)
        def _(i):
            ref = got.at[which, (t + 16 - i) % 16]
            pltpu.make_async_remote_copy(
                src_ref=ref, dst_ref=ref, send_sem=fin_s.at[which, i], recv_sem=fin_r.at[which, i],
                device_id=core_pair, device_id_type=MESH,
            ).wait_recv()

        @pl.loop(0, 8)
        def _(k):
            for n, (dx, dz) in enumerate(offsets):
                chip = (k // 2) * 2 + (k % 2 + dz) % 2
                cols = pl.ds(pl.multiple_of((fsdp_slot(dx, dz) * 8 + chip) * 128, 128), 128)
                part = slice(n * 128, (n + 1) * 128)
                both = got[which, k * 2, :, part].astype(F32) + got[which, k * 2 + 1, :, part].astype(F32)
                out_ref[:, cols] = (both * os_ref[:, cols]).astype(BF16)

    collect(0, ((0, 0), (1, 0), (3, 0), (0, 1)))
    collect(1, ((2, 0), (1, 1), (3, 1), (2, 1)))

    @pl.loop(1, 16)
    def _(i):
        block_copy(i).wait_send()
        final_copy(0, i).wait_send()
        final_copy(1, i).wait_send()

    core_w.wait_send()
    core_kv.wait_send()
    out_gather.sent()
    in_gather.sent()
    att_gather.sent()


def shards(
    hidden_in, lengths, norm_gain, query_weight, key_weight, value_weight, out_weight,
    query_scale, key_scale, value_scale, out_scale,
):
    vmem = pl.BlockSpec(memory_space=pltpu.VMEM)
    any_space = pl.BlockSpec(memory_space=pl.ANY)
    smem = pl.BlockSpec(memory_space=pltpu.SMEM)
    dma = pltpu.SemaphoreType.DMA
    return pl.pallas_call(
        kernel,
        out_shape=jax.ShapeDtypeStruct((32, D), BF16),
        in_specs=[any_space, smem, vmem, any_space, any_space, any_space, any_space, vmem, vmem, vmem, vmem],
        out_specs=vmem,
        scratch_shapes=[
            pltpu.VMEM((TOK, D), BF16),
            pltpu.VMEM((64, D), BF16),
            pltpu.VMEM((64, 1024), BF16),
            pltpu.VMEM((64, 1024), BF16),
            pltpu.VMEM((D, 64), BF16),
            pltpu.VMEM((16, 64, 640), BF16),
            pltpu.VMEM((8, 1024, 640), BF16),
            pltpu.VMEM((8, 4096, 128), BF16),
            pltpu.VMEM((4096, 128), BF16),
            pltpu.VMEM((4096, 128), BF16),
            pltpu.VMEM((4096, 128), BF16),
            pltpu.VMEM((TOK, 640), F32),
            pltpu.VMEM((TOK, HD), F32),
            pltpu.VMEM((TOK, HD), F32),
            pltpu.VMEM((TOK, HD), jnp.int32),
            pltpu.VMEM((4, TOK, HD), BF16),
            pltpu.VMEM((2, TOK, HD), BF16),
            pltpu.VMEM((8, 2, TOK, 256), BF16),
            pltpu.VMEM((2, TOK, 512), F32),
            pltpu.VMEM((2, TOK, 512), BF16),
            pltpu.VMEM((2, 16, 32, 512), BF16),
            dma((5,)), dma((16,)), dma((16,)), dma((2,)), dma((2,)),
            dma((2, 8)), dma((2, 8)), dma((2, 8)), dma((2, 8)), dma((2, 8)), dma((2, 8)),
            dma((2, 16)), dma((2, 16)),
        ],
        compiler_params=pltpu.CompilerParams(
            collective_id=0, has_side_effects=True, vmem_limit_bytes=60 * 1024 * 1024
        ),
        cost_estimate=pl.CostEstimate(flops=10_000_000_000, bytes_accessed=16_000_000, transcendentals=1_000_000),
        name="refresh_and_prefill",
    )(
        hidden_in, lengths, norm_gain.reshape(1, -1), query_weight, key_weight, value_weight, out_weight,
        query_scale.reshape(1, -1), key_scale.reshape(1, -1), value_scale.reshape(1, -1), out_scale.reshape(1, -1),
    )


def solution(mesh):
    in_specs = (
        P("fsdp", None),
        P("fsdp", None),
        P(),
        P(("fsdp", "tp"), None),
        P(("fsdp", "tp"), None),
        P(("fsdp", "tp"), None),
        P(None, ("fsdp", "tp")),
        P(),
        P(),
        P(),
        P(),
    )
    return jax.shard_map(
        shards, mesh=mesh, in_specs=in_specs, out_specs=P(("fsdp", "tp"), None), check_vma=False
    )
```

time: 718 us -> 176 us (0.25)
  waiting for transfers between devices: 523 us -> 0 us
  Pallas kernels: 0 us -> 172 us
  local copies, waits for them, and re-layouts: 92.5 us -> 4.65 us
  matrix products: 40 us -> 0 us
  starting transfers between devices: 24.2 us -> 0 us
  other arithmetic: 23.2 us -> 0 us
  between operations: 13.3 us -> 0.01 us
    all_gather x4 -> x0, waiting for transfers between devices: 368 us -> none  [the longest x1 167 us: shards(): out_cols = lax.all_gather(out_cast, 'fsdp', axis=1, tiled=True)]
    pallas_call x0 -> x1, Pallas kernels: none -> 172 us  [shards(): pl.pallas_call(kernel, out_shape=jax.ShapeDtypeStruct((32, D), BF16), in_...]
    reduce_scatter x1 -> x0, waiting for transfers between devices: 98.6 us -> none  [shards(): lax.psum_scatter(jnp.dot(attended, out_local, preferred_element_type=jnp....]
    all_to_all x4 -> x0, waiting for transfers between devices: 56.3 us -> none  [the longest x1 56.3 us: shards(): lax.all_to_all(out_cols, 'tp', split_axis=0, concat_axis=1, tiled=True)]
    dot_general x5 -> x0, matrix products: 40 us -> none  [the longest x1 12.8 us: shards(): query_proj = jnp.dot(normed, query_full, preferred_element_type=jnp.float32)]
    all_gather x4 -> x0, local copies, waits for them, and re-layouts: 28.1 us -> none  [the longest x1 12 us: shards(): out_cols = lax.all_gather(out_cast, 'fsdp', axis=1, tiled=True)]
    all_to_all x2 -> x0, local copies, waits for them, and re-layouts: 24.7 us -> none  [the longest x1 12.3 us: shards(): lax.all_to_all(out_cols, 'tp', split_axis=0, concat_axis=1, tiled=True)]
    all_to_all x4 -> x0, starting transfers between devices: 23.2 us -> none  [the longest x1 5.97 us: shards(): lax.all_to_all(value_rows, 'tp', split_axis=1, concat_axis=0, tiled=True)]
  transfers between devices with their start and end apart: 11 -> 0, of which waited for: 6 -> 0; matrix products, arithmetic and copies ran while one was open for 15% -> 0% of each run, Pallas kernels for 0% -> 0%
where the time goes in v1:
time: 176 us
  Pallas kernels  172 us (98%)
  local copies, waits for them, and re-layouts  4.65 us (3%)
    pallas_call x1, Pallas kernels, shards(): pl.pallas_call(kernel, out_shape=jax.ShapeDtypeStruct((32, D), BF16), in_...  172 us
    unnamed x2, local copies, waits for them, and re-layouts  4.65 us

profile of v1, /device:TPU:1, one launch (start us, length us, event | category | flops | bytes accessed | tf_op | source)
XLA Modules:
  0.0 176.2 jit_solution(14902422955513197813)
XLA Ops:
  0.0 2.8 %copy.12.wo_ref = bf16[8192,64]{1,0:T(8,128)(2,1)} copy(bf16[8192,64]{0,1:T(8,128)(2,1)} %param.17) | data formatting | bytes 2097152 | tf_op args[6]
  2.8 171.5 %refresh_and_prefill.1 = bf16[32,8192]{1,0:T(8,128)(2,1)} custom-call(bf16[512,8192]{1,0:T(8,128)(2,1)} %hidden_ref.1, s32[1,8]{1,0:T(1,128)} %lengths_ref.1, f32[1,8192]{1,0:T(1,128)} %bitcast.5, bf16[64,8192]{1,0:T(8,128)(2,1)} %wq_ref.1, bf16[64,1024]{1,0:T(8,128)(2,1)} %wk_ref.1, bf16[64,1024]{1,0:T(8,128)(2,1)} %wv_ref.1, ...), custom_call_target="tpu_custom_call" | custom-call | flops 10000000000 | bytes 16000000 | tf_op jit(solution)/shard_map/refresh_and_prefill/pallas_call | solution.py:441
  174.3 1.9 %copy.14 = bf16[32,8192]{1,0:T(8,128)(2,1)} copy(bf16[32,8192]{1,0:T(8,128)(2,1)} %refresh_and_prefill.1) | data formatting | bytes 1048576

commit v2 on v1

v2 whole, which is shorter than its diff:
```python
import math

import jax
import jax.numpy as jnp
from jax import lax
from jax.experimental import pallas as pl
from jax.experimental.pallas import tpu as pltpu
from jax.sharding import PartitionSpec as P

MESH = pl.DeviceIdType.MESH
F32 = jnp.float32
BF16 = jnp.bfloat16

HD = 128
TOK = 512
D = 8192
SATURATE = 448.0
EPSILON = 1e-06
ROPE_BASE = 1000000.0
MASKED_SCORE = -1e30

OUT_TREE = {
    (1, 0): (0, 0, 1),
    (3, 0): (0, 0, -1),
    (0, 1): (0, 0, 0),
    (2, 0): (1, 0, 1),
    (2, 1): (2, 0, 0),
    (1, 1): (0, 1, 1),
    (3, 1): (0, 1, -1),
}
IN_TREE = {**OUT_TREE, (2, 1): (1, 1, 1)}
RING = {(1, 0): (0, 0, 1), (3, 0): (0, 0, -1), (2, 0): (1, 0, 1)}


class Gather:
    def __init__(self, tree, slot, piece, send_sem, recv_sem, plus, minus, pair, source=None):
        self.tree, self.slot, self.piece = tree, slot, piece
        self.send_sem, self.recv_sem = send_sem, recv_sem
        self.to = {1: plus, -1: minus, 0: pair}
        self.source = source

    def index(self, u, dz, h):
        return self.slot(u if h == 0 else (4 - u) % 4, dz)

    def ref(self, u, dz, h):
        return self.piece(self.index(u, dz, h), h)

    def copy(self, u, dz, h):
        su, sdz, step = self.tree[(u, dz)]
        here = there = self.ref(su, sdz, h)
        if self.source is not None and (su, sdz) == (0, 0):
            here = self.source(h, step)
        return pltpu.make_async_remote_copy(
            src_ref=here,
            dst_ref=there,
            send_sem=self.send_sem.at[h, u * 2 + dz],
            recv_sem=self.recv_sem.at[h, u * 2 + dz],
            device_id=self.to[step if h == 0 else -step],
            device_id_type=MESH,
        )

    def send(self, h, *targets):
        for u, dz in targets:
            self.copy(u, dz, h).start()

    def arrived(self, u, dz, h):
        ref = self.ref(u, dz, h)
        pltpu.make_async_remote_copy(
            src_ref=ref,
            dst_ref=ref,
            send_sem=self.send_sem.at[h, u * 2 + dz],
            recv_sem=self.recv_sem.at[h, u * 2 + dz],
            device_id=self.to[1],
            device_id_type=MESH,
        ).wait_recv()

    def sent(self):
        for h in range(2):
            for u, dz in self.tree:
                self.copy(u, dz, h).wait_send()


class Across:
    def __init__(self, gather, piece, send_sem, recv_sem, core_pair):
        self.gather, self.piece = gather, piece
        self.send_sem, self.recv_sem, self.core_pair = send_sem, recv_sem, core_pair
        self.keys = [(0, 0), *gather.tree]

    def copy(self, u, dz, h, other):
        ref = self.piece(self.gather.index(u, dz, h), h, other)
        return pltpu.make_async_remote_copy(
            src_ref=ref, dst_ref=ref, send_sem=self.send_sem.at[h, u * 2 + dz], recv_sem=self.recv_sem.at[h, u * 2 + dz],
            device_id=self.core_pair, device_id_type=MESH,
        )

    def send(self, u, dz, h):
        self.copy(u, dz, h, False).start()

    def arrived(self, u, dz, h):
        self.copy(u, dz, h, True).wait_recv()

    def sent(self):
        for h in range(2):
            for u, dz in self.keys:
                self.copy(u, dz, h, False).wait_send()


def choose(i, values):
    result = values[-1]
    for n in range(len(values) - 2, -1, -1):
        result = jnp.where(i == n, values[n], result)
    return result


def kernel(
    hidden_ref, lengths_ref, gain_ref, wq_ref, wk_ref, wv_ref, wo_ref, qs_ref, ks_ref, vs_ref, os_ref,
    out_ref,
    nrm, raw_q, raw_k, raw_v, raw_o, snd, w_own, w_in, wo, len_t, acc_a, acc_b, cos_t, sin_t, begin_t,
    q_t, kv_t, att_out, att, acc_o, ost, got,
    load_sem, a2a_s, a2a_r, one_s, one_r, core_s, core_r, rows_s, rows_r, ring_s, ring_r, racross_s, racross_r,
    q_s, q_r, o_s, o_r, att_s, att_r, across_s, across_r, fin_s, fin_r,
):
    f = lax.axis_index("fsdp")
    t = lax.axis_index("tp")
    x, zh = f // 2, f % 2
    y, zl, c = t // 4, (t // 2) % 2, t % 2
    rz = (zl + zh) % 2
    role = y * 2 + rz
    hb = role * 2 + c

    def device(ff, tt):
        return {"fsdp": ff, "tp": tt}

    x_plus = device(((x + 1) % 4) * 2 + zh, t)
    x_minus = device(((x + 3) % 4) * 2 + zh, t)
    z_pair = device(x * 2 + 1 - zh, y * 4 + (1 - zl) * 2 + c)
    y_plus = device(f, ((y + 1) % 4) * 4 + zl * 2 + c)
    y_minus = device(f, ((y + 3) % 4) * 4 + zl * 2 + c)
    zl_pair = device(f, y * 4 + (1 - zl) * 2 + c)
    core_pair = device(f, y * 4 + zl * 2 + 1 - c)

    barrier = pltpu.get_barrier_semaphore()
    for other in (x_plus, x_minus, z_pair):
        pl.semaphore_signal(barrier, inc=1, device_id=other, device_id_type=MESH)

    @pl.loop(1, 16)
    def _(i):
        pl.semaphore_signal(barrier, inc=1, device_id=device(f, (t + i) % 16), device_id_type=MESH)

    loads = [
        pltpu.make_async_copy(src, dst, load_sem.at[n])
        for n, (src, dst) in enumerate([(wq_ref, raw_q), (wk_ref, raw_k), (wv_ref, raw_v), (wo_ref, raw_o)])
    ]
    for j in range(8):
        loads.append(pltpu.make_async_copy(hidden_ref.at[:, pl.ds(j * 1024, 1024)], nrm.at[0, j], load_sem.at[4 + j]))
    for load in loads:
        load.start()

    def quantize(weight, inverse):
        return jnp.clip(weight.astype(F32) * inverse, -SATURATE, SATURATE).astype(BF16)

    for load in loads[:3]:
        load.wait()

    @pl.loop(0, 8)
    def _(r):
        for n in range(2):
            for part, place in ((zh, slice(0, 256)), (1 - zh, slice(384, 640))):
                cols = pl.ds(pl.multiple_of((r * 2 + n) * 512 + part * 256, 256), 256)
                snd[r * 2 + n, :, place] = quantize(raw_q[:, cols], 1.0 / qs_ref[:, cols])
        cols = pl.ds(pl.multiple_of(r * 128, 128), 128)
        snd[r * 2, :, 256:384] = quantize(raw_k[:, cols], 1.0 / ks_ref[:, cols])
        snd[r * 2 + 1, :, 256:384] = quantize(raw_v[:, cols], 1.0 / vs_ref[:, cols])

    for n in range(8):
        len_t[0, n:n + 1, :] = jnp.full((1, 128), lengths_ref[0, n], jnp.int32)

    pl.semaphore_wait(barrier, 18)

    def block_copy(i):
        to = (t + i) % 16
        block = ((to // 4) * 2 + ((to // 2) % 2 + zh) % 2) * 2 + to % 2
        return pltpu.make_async_remote_copy(
            src_ref=snd.at[block],
            dst_ref=w_own.at[pl.ds(pl.multiple_of(t * 64, 64), 64)],
            send_sem=a2a_s.at[i],
            recv_sem=a2a_r.at[i],
            device_id=device(f, to),
            device_id_type=MESH,
        )

    @pl.loop(1, 16)
    def _(i):
        block_copy(i).start()

    w_own[pl.ds(pl.multiple_of(t * 64, 64), 64)] = snd[hb]

    def one_copy(n, src, dst, device_id):
        return pltpu.make_async_remote_copy(
            src_ref=src, dst_ref=dst, send_sem=one_s.at[n], recv_sem=one_r.at[n],
            device_id=device_id, device_id_type=MESH,
        )

    len_copy = one_copy(0, len_t.at[0], len_t.at[1], z_pair)
    len_copy.start()

    loads[3].wait()
    chip_cols = pl.ds(pl.multiple_of((f * 8 + t // 2) * 128, 128), 128)
    chip_scale = jnp.broadcast_to(1.0 / os_ref[:, chip_cols], (128, 128))
    on_diagonal = lax.broadcasted_iota(jnp.int32, (128, 128), 0) == lax.broadcasted_iota(jnp.int32, (128, 128), 1)
    chip_column = jnp.sum(jnp.where(on_diagonal, chip_scale, 0.0), axis=1, keepdims=True)
    own_scale = jnp.where(c == 0, chip_column[:64], chip_column[64:])

    @pl.loop(0, 16)
    def _(i):
        cols = pl.ds(pl.multiple_of(i * 512, 512), 512)
        wo[f, :, cols] = quantize(raw_o[:, cols], own_scale)

    def fsdp_slot(dx, dz):
        return ((x + 4 - dx) % 4) * 2 + (zh + dz) % 2

    out_gather = Gather(
        OUT_TREE, fsdp_slot, lambda s, h: wo.at[s, pl.ds(h * 32, 32)], o_s, o_r, x_plus, x_minus, z_pair
    )
    in_gather = Gather(
        IN_TREE, fsdp_slot, lambda s, h: w_in.at[s, pl.ds(h * 512, 512)], q_s, q_r, x_plus, x_minus, z_pair,
        lambda h, step: w_own.at[pl.ds(h * 512, 512), pl.ds(0 if step else 256, 384)],
    )
    row_gather = Gather(
        RING, lambda dy, dz: ((y + 4 - dy) % 4) * 2,
        lambda s, h: nrm.at[1, s + c, pl.ds(h * 256, 256)], ring_s, ring_r, y_plus, y_minus, zl_pair,
    )
    row_across = Across(
        row_gather, lambda s, h, other: nrm.at[1, s + (1 - c if other else c), pl.ds(h * 256, 256)],
        racross_s, racross_r, core_pair,
    )
    att_gather = Gather(
        OUT_TREE, lambda dy, dz: ((y + 4 - dy) % 4) * 2 + (rz + dz) % 2,
        lambda s, h: att.at[s * 2 + c, (zh + h) % 2], att_s, att_r, y_plus, y_minus, zl_pair,
    )
    att_across = Across(
        att_gather, lambda s, h, other: att.at[s * 2 + (1 - c if other else c), (zh + h) % 2],
        across_s, across_r, core_pair,
    )
    for h in range(2):
        out_gather.send(h, (1, 0), (3, 0))

    for load in loads[4:]:
        load.wait()

    def row_copy(h):
        rows = pl.ds(h * 256, 256)
        return pltpu.make_async_remote_copy(
            src_ref=nrm.at[0, y * 2 + c, rows], dst_ref=nrm.at[1, y * 2 + c, rows],
            send_sem=rows_s.at[h], recv_sem=rows_r.at[h], device_id=z_pair, device_id_type=MESH,
        )

    for h in range(2):
        @pl.loop(h * 16, h * 16 + 16)
        def _(i):
            rows = pl.ds(pl.multiple_of(i * 16, 16), 16)
            square = jnp.zeros((16, 1024), F32)
            for j in range(8):
                wide = nrm[0, j, rows, :].astype(F32)
                square += wide * wide
            inverse = lax.rsqrt(jnp.sum(square, axis=1, keepdims=True) * (1.0 / D) + EPSILON)
            for j in range(8):
                wide = nrm[0, j, rows, :].astype(F32)
                nrm[0, j, rows, :] = (wide * inverse * gain_ref[:, j * 1024:(j + 1) * 1024]).astype(BF16)

        row_copy(h).start()

    place = lax.broadcasted_iota(jnp.int32, (TOK, 128), 0)
    lane = lax.broadcasted_iota(jnp.int32, (TOK, 128), 1)

    def tables(replica):
        begin = jnp.zeros((TOK, 128), jnp.int32)
        start = jnp.zeros((1, 128), jnp.int32)
        for n in range(8):
            begin = jnp.where(place >= start, start, begin)
            start = start + len_t[replica, n:n + 1, :]
        begin_t[replica] = begin
        frequency = jnp.exp((lane % 64).astype(F32) * (-2.0 * math.log(ROPE_BASE) / HD))
        angle = (place - begin).astype(F32) * frequency
        cos_t[replica] = jnp.cos(angle)
        sine = jnp.sin(angle)
        sin_t[replica] = jnp.where(lane < 64, -sine, sine)

    tables(0)
    len_copy.wait_recv()
    tables(1)

    for h in range(2):
        @pl.loop(h * 8, h * 8 + 8)
        def _(src):
            @pl.when(src != t)
            def _():
                ref = w_own.at[pl.ds(pl.multiple_of(src * 64, 64), 64)]
                i = (t + 16 - src) % 16
                pltpu.make_async_remote_copy(
                    src_ref=ref, dst_ref=ref, send_sem=a2a_s.at[i], recv_sem=a2a_r.at[i],
                    device_id=core_pair, device_id_type=MESH,
                ).wait_recv()

        in_gather.send(h, (1, 0), (3, 0), (0, 1))

    acc_a[...] = jnp.zeros_like(acc_a)
    acc_b[...] = jnp.zeros_like(acc_b)

    def project(replica, *pieces):
        for dz, total in ((0, acc_a), (1, acc_b)):
            some = [(u, h) for u, z, h in pieces if z == dz and (u, z) != (0, 0)]
            if not some:
                continue
            slots, halves = [in_gather.index(u, dz, h) for u, h in some], [h for _, h in some]

            @pl.loop(0, len(some))
            def _(i):
                s, h = choose(i, slots), choose(i, halves)
                cols = pl.ds(pl.multiple_of(h * 512, 512), 512)
                total[replica] += jnp.dot(nrm[replica, s, :, cols], w_in[s, cols, :], preferred_element_type=F32)

    def project_own(replica):
        @pl.loop(0, 2)
        def _(h):
            cols = pl.ds(pl.multiple_of(h * 512, 512), 512)
            acc_a[replica] += jnp.dot(nrm[replica, f, :, cols], w_own[cols, 0:384], preferred_element_type=F32)

    def halves_of(*places):
        return [(u, dz, h) for u, dz in places for h in range(2)]

    project_own(0)
    for h in range(2):
        row_copy(h).wait_recv()
        row_gather.send(h, (1, 0), (3, 0))
        row_across.send(0, 0, h)
    for h in range(2):
        in_gather.arrived(1, 0, h)
        in_gather.send(h, (2, 0))
    project(0, *halves_of((1, 0)))
    for h in range(2):
        row_gather.arrived(1, 0, h)
        row_gather.send(h, (2, 0))
        row_across.send(1, 0, h)
    for h in range(2):
        in_gather.arrived(0, 1, h)
        in_gather.send(h, (1, 1), (3, 1))
        out_gather.send(h, (0, 1))
    for h in range(2):
        in_gather.arrived(3, 0, h)
    project(0, *halves_of((0, 1), (3, 0)))
    for h in range(2):
        row_gather.arrived(3, 0, h)
        row_across.send(3, 0, h)
    for h in range(2):
        in_gather.arrived(2, 0, h)
    project(0, *halves_of((2, 0)))
    for h in range(2):
        in_gather.arrived(1, 1, h)
        in_gather.send(h, (2, 1))
    project(0, *halves_of((1, 1)))
    for h in range(2):
        row_gather.arrived(2, 0, h)
        row_across.send(2, 0, h)
    for h in range(2):
        for u in range(4):
            row_across.arrived(u, 0, h)
    project_own(1)
    project(1, *halves_of((1, 0), (3, 0), (2, 0), (0, 1), (1, 1)))
    for h in range(2):
        in_gather.arrived(3, 1, h)
    for h in range(2):
        out_gather.arrived(1, 0, h)
        out_gather.send(h, (2, 0))
    for replica in range(2):
        project(replica, *halves_of((3, 1)))
    for h in range(2):
        in_gather.arrived(2, 1, h)
    for h in range(2):
        out_gather.arrived(0, 1, h)
        out_gather.send(h, (1, 1), (3, 1))
    for replica in range(2):
        project(replica, *halves_of((2, 1)))

    def rope(v, replica):
        return v * cos_t[replica] + pltpu.roll(v, 64, axis=1) * sin_t[replica]

    def core_copy(replica, core):
        return pltpu.make_async_remote_copy(
            src_ref=kv_t.at[replica, core], dst_ref=kv_t.at[replica, core],
            send_sem=core_s.at[replica], recv_sem=core_r.at[replica],
            device_id=core_pair, device_id_type=MESH,
        )

    kv_cols = pl.ds(pl.multiple_of(role * 128, 128), 128)
    for replica in (1, 0):
        product = acc_a[replica, :, 256:384] + acc_b[replica, :, 0:128]
        key_raw = (product * ks_ref[:, kv_cols]).astype(BF16).astype(F32)
        value = product * vs_ref[:, kv_cols]
        kv_t[replica, c] = jnp.where(c == 0, rope(key_raw, replica), value).astype(BF16)
        core_copy(replica, c).start()

    for replica in (1, 0):
        for n in range(2):
            product = acc_a[replica, :, n * 128:(n + 1) * 128] + acc_b[replica, :, (n + 1) * 128:(n + 2) * 128]
            scale = qs_ref[:, pl.ds(pl.multiple_of(hb * 512 + zh * 256 + n * 128, 128), 128)]
            q_t[replica, n] = rope(product * scale, replica).astype(BF16)

    def attend(replica, out):
        for n in range(2):
            for b in range(4):
                first = max(0, b * 128 - 256)
                width = (b + 1) * 128 - first
                rows = slice(b * 128, (b + 1) * 128)
                keys = slice(first, first + width)
                scores = lax.dot_general(
                    q_t[replica, n, rows], kv_t[replica, 0, keys], (((1,), (1,)), ((), ())), preferred_element_type=F32
                ) * HD ** (-0.5)
                p = lax.broadcasted_iota(jnp.int32, (128, width), 0) + b * 128
                s = lax.broadcasted_iota(jnp.int32, (128, width), 1) + first
                keep = (s <= p) & (s >= begin_t[replica, rows, 0:1])
                scores = jnp.where(keep, scores, MASKED_SCORE)
                weights = jnp.exp(scores - jnp.max(scores, axis=1, keepdims=True))
                total = jnp.sum(weights, axis=1, keepdims=True)
                mixed = jnp.dot(weights.astype(BF16), kv_t[replica, 1, keys], preferred_element_type=F32)
                out[rows, n * 128:(n + 1) * 128] = (mixed / total).astype(BF16)

    core_copy(1, 1 - c).wait_recv()
    attend(1, att_out)
    att_copy = one_copy(1, att_out, att.at[hb, zh], z_pair)
    att_copy.start()
    core_copy(0, 1 - c).wait_recv()
    attend(0, att.at[hb, zh])
    att_gather.send(0, (1, 0), (3, 0), (0, 1))
    att_across.send(0, 0, 0)
    one_copy(1, att_out, att.at[hb, 1 - zh], z_pair).wait_recv()
    att_gather.send(1, (1, 0), (3, 0), (0, 1))
    att_across.send(0, 0, 1)

    def take(u, dz, h):
        att_gather.arrived(u, dz, h)
        att_across.send(u, dz, h)

    early = [fsdp_slot(dx, dz) for dx, dz in ((0, 0), (1, 0), (3, 0), (0, 1))]
    late = [fsdp_slot(dx, dz) for dx, dz in ((2, 0), (1, 1), (3, 1), (2, 1))]

    def mix(which, slots, pieces):
        roles = [att_gather.index(u, dz, h) for u, dz, h in pieces]
        halves = [(zh + h) % 2 for _, _, h in pieces]
        if which == 0:
            for u, dz, h in pieces:
                att_across.arrived(u, dz, h)

        @pl.loop(0, len(pieces))
        def _(i):
            r, h = choose(i, roles), choose(i, halves)
            for n in range(2):
                cols = pl.ds(pl.multiple_of(r * 1024 + n * 512 + h * 256, 256), 256)
                columns = jnp.concatenate([wo[s, :, cols] for s in slots], axis=0)
                acc_o[which] += lax.dot_general(
                    att[r * 2 + n, h], columns, (((1,), (1,)), ((), ())), preferred_element_type=F32
                )

    def finish(which):
        ost[which] = acc_o[which].astype(BF16)

        @pl.loop(1, 16)
        def _(i):
            final_copy(which, i).start()

        got[which, t] = ost[which, pl.ds(pl.multiple_of(t * 32, 32), 32)]

    def final_copy(which, i):
        to = (t + i) % 16
        return pltpu.make_async_remote_copy(
            src_ref=ost.at[which, pl.ds(pl.multiple_of(to * 32, 32), 32)],
            dst_ref=got.at[which, t],
            send_sem=fin_s.at[which, i],
            recv_sem=fin_r.at[which, i],
            device_id=device(f, to),
            device_id_type=MESH,
        )

    acc_o[...] = jnp.zeros_like(acc_o)
    for h in range(2):
        out_gather.arrived(3, 0, h)
    mix(0, early, [(0, 0, 0), (0, 0, 1)])
    for h in range(2):
        take(1, 0, h)
        att_gather.send(h, (2, 0))
        take(0, 1, h)
        att_gather.send(h, (1, 1), (3, 1))
    mix(0, early, [(1, 0, 0), (1, 0, 1), (0, 1, 0), (0, 1, 1)])
    for h in range(2):
        out_gather.arrived(2, 0, h)
        out_gather.send(h, (2, 1))
    for h in range(2):
        take(3, 0, h)
    for h in range(2):
        take(2, 0, h)
        att_gather.send(h, (2, 1))
    mix(0, early, [(3, 0, 0), (3, 0, 1), (2, 0, 0), (2, 0, 1)])
    for h in range(2):
        for u in (1, 3, 2):
            take(u, 1, h)
    mix(0, early, [(u, 1, h) for u in (1, 3, 2) for h in range(2)])
    finish(0)
    for h in range(2):
        for u in (1, 3, 2):
            out_gather.arrived(u, 1, h)
    mix(1, late, [(u, dz, h) for u in range(4) for dz in range(2) for h in range(2)])
    finish(1)

    def collect(which, offsets):
        @pl.loop(1, 16)
        def _(i):
            ref = got.at[which, (t + 16 - i) % 16]
            pltpu.make_async_remote_copy(
                src_ref=ref, dst_ref=ref, send_sem=fin_s.at[which, i], recv_sem=fin_r.at[which, i],
                device_id=core_pair, device_id_type=MESH,
            ).wait_recv()

        @pl.loop(0, 8)
        def _(k):
            for n, (dx, dz) in enumerate(offsets):
                chip = (k // 2) * 2 + (k % 2 + dz) % 2
                cols = pl.ds(pl.multiple_of((fsdp_slot(dx, dz) * 8 + chip) * 128, 128), 128)
                part = slice(n * 64, (n + 1) * 64)
                both = jnp.concatenate([got[which, k * 2, :, part], got[which, k * 2 + 1, :, part]], axis=1)
                out_ref[:, cols] = (both.astype(F32) * os_ref[:, cols]).astype(BF16)

    collect(0, ((0, 0), (1, 0), (3, 0), (0, 1)))
    collect(1, ((2, 0), (1, 1), (3, 1), (2, 1)))

    @pl.loop(1, 16)
    def _(i):
        block_copy(i).wait_send()
        final_copy(0, i).wait_send()
        final_copy(1, i).wait_send()

    len_copy.wait_send()
    att_copy.wait_send()
    for n in range(2):
        core_copy(n, c).wait_send()
        row_copy(n).wait_send()
    for group in (out_gather, in_gather, row_gather, row_across, att_gather, att_across):
        group.sent()


def shards(
    hidden_in, lengths, norm_gain, query_weight, key_weight, value_weight, out_weight,
    query_scale, key_scale, value_scale, out_scale,
):
    vmem = pl.BlockSpec(memory_space=pltpu.VMEM)
    any_space = pl.BlockSpec(memory_space=pl.ANY)
    smem = pl.BlockSpec(memory_space=pltpu.SMEM)
    dma = pltpu.SemaphoreType.DMA
    return pl.pallas_call(
        kernel,
        out_shape=jax.ShapeDtypeStruct((32, D), BF16),
        in_specs=[any_space, smem, vmem, any_space, any_space, any_space, any_space, vmem, vmem, vmem, vmem],
        out_specs=vmem,
        scratch_shapes=[
            pltpu.VMEM((2, 8, TOK, 1024), BF16),
            pltpu.VMEM((64, D), BF16),
            pltpu.VMEM((64, 1024), BF16),
            pltpu.VMEM((64, 1024), BF16),
            pltpu.VMEM((64, D), BF16),
            pltpu.VMEM((16, 64, 640), BF16),
            pltpu.VMEM((1024, 640), BF16),
            pltpu.VMEM((8, 1024, 384), BF16),
            pltpu.VMEM((8, 64, D), BF16),
            pltpu.VMEM((2, 8, 128), jnp.int32),
            pltpu.VMEM((2, TOK, 384), F32),
            pltpu.VMEM((2, TOK, 384), F32),
            pltpu.VMEM((2, TOK, HD), F32),
            pltpu.VMEM((2, TOK, HD), F32),
            pltpu.VMEM((2, TOK, HD), jnp.int32),
            pltpu.VMEM((2, 2, TOK, HD), BF16),
            pltpu.VMEM((2, 2, TOK, HD), BF16),
            pltpu.VMEM((TOK, 256), BF16),
            pltpu.VMEM((16, 2, TOK, 256), BF16),
            pltpu.VMEM((2, TOK, 256), F32),
            pltpu.VMEM((2, TOK, 256), BF16),
            pltpu.VMEM((2, 16, 32, 256), BF16),
            dma((12,)), dma((16,)), dma((16,)), dma((2,)), dma((2,)), dma((2,)), dma((2,)), dma((2,)), dma((2,)),
            dma((2, 8)), dma((2, 8)), dma((2, 8)), dma((2, 8)),
            dma((2, 8)), dma((2, 8)), dma((2, 8)), dma((2, 8)), dma((2, 8)), dma((2, 8)), dma((2, 8)), dma((2, 8)),
            dma((2, 16)), dma((2, 16)),
        ],
        compiler_params=pltpu.CompilerParams(
            collective_id=0, has_side_effects=True, vmem_limit_bytes=60 * 1024 * 1024
        ),
        cost_estimate=pl.CostEstimate(flops=10_000_000_000, bytes_accessed=16_000_000, transcendentals=1_000_000),
        name="refresh_and_prefill",
    )(
        hidden_in, lengths, norm_gain.reshape(1, -1), query_weight, key_weight, value_weight, out_weight.T,
        query_scale.reshape(1, -1), key_scale.reshape(1, -1), value_scale.reshape(1, -1), out_scale.reshape(1, -1),
    )


def solution(mesh):
    in_specs = (
        P("fsdp", None),
        P("fsdp", None),
        P(),
        P(("fsdp", "tp"), None),
        P(("fsdp", "tp"), None),
        P(("fsdp", "tp"), None),
        P(None, ("fsdp", "tp")),
        P(),
        P(),
        P(),
        P(),
    )
    return jax.shard_map(
        shards, mesh=mesh, in_specs=in_specs, out_specs=P(("fsdp", "tp"), None), check_vma=False
    )
```

time: 176 us -> 153 us (0.87)
  Pallas kernels: 172 us -> 151 us
  local copies, waits for them, and re-layouts: 4.65 us -> 1.87 us
    pallas_call x1, Pallas kernels: 172 us -> 151 us  [shards(): pl.pallas_call(kernel, out_shape=jax.ShapeDtypeStruct((32, D), BF16), in_...]
    unnamed x2 -> x1, local copies, waits for them, and re-layouts: 4.65 us -> 1.87 us
where the time goes in v2:
time: 153 us
  Pallas kernels  151 us (99%)
  local copies, waits for them, and re-layouts  1.87 us (1%)
    pallas_call x1, Pallas kernels, shards(): pl.pallas_call(kernel, out_shape=jax.ShapeDtypeStruct((32, D), BF16), in_...  151 us

profile of v2, /device:TPU:1, one launch (start us, length us, event | category | flops | bytes accessed | tf_op | source)
XLA Modules:
  0.0 152.9 jit_solution(2869500480865925848)
XLA Ops:
  0.0 151.0 %refresh_and_prefill.1 = bf16[32,8192]{1,0:T(8,128)(2,1)} custom-call(bf16[512,8192]{1,0:T(8,128)(2,1)} %hidden_ref.1, s32[1,8]{1,0:T(1,128)} %lengths_ref.1, f32[1,8192]{1,0:T(1,128)} %bitcast.7, bf16[64,8192]{1,0:T(8,128)(2,1)} %wq_ref.1, bf16[64,1024]{1,0:T(8,128)(2,1)} %wk_ref.1, bf16[64,1024]{1,0:T(8,128)(2,1)} %wv_ref.1, bf16[64,8192]{1,0:T(8,128)(2,1)} %bitcast.6, ...), custom_call_target="tpu_custom_call" | custom-call | flops 10000000000 | bytes 16000000 | tf_op jit(solution)/shard_map/refresh_and_prefill/pallas_call | solution.py:558
  151.0 1.9 %copy.13 = bf16[32,8192]{1,0:T(8,128)(2,1)} copy(bf16[32,8192]{1,0:T(8,128)(2,1)} %refresh_and_prefill.1) | data formatting | bytes 1048576

commit v3 on v2

v3 whole, which is shorter than its diff:
```python
import math

import jax
import jax.numpy as jnp
from jax import lax
from jax.experimental import pallas as pl
from jax.experimental.pallas import tpu as pltpu
from jax.sharding import PartitionSpec as P

MESH = pl.DeviceIdType.MESH
F32 = jnp.float32
BF16 = jnp.bfloat16

HD = 128
TOK = 512
D = 8192
SATURATE = 448.0
EPSILON = 1e-06
ROPE_BASE = 1000000.0
MASKED_SCORE = -1e30

OUT_TREE = {
    (1, 0): (0, 0, 1),
    (3, 0): (0, 0, -1),
    (0, 1): (0, 0, 0),
    (2, 0): (1, 0, 1),
    (2, 1): (2, 0, 0),
    (1, 1): (0, 1, 1),
    (3, 1): (0, 1, -1),
}
PAIR_TREE = {**OUT_TREE, (3, 1): (3, 0, 0)}
IN_TREE = {**OUT_TREE, (2, 1): (1, 1, 1)}


class Gather:
    def __init__(self, trees, slot, piece, send_sem, recv_sem, plus, minus, pair, source=None):
        self.trees, self.slot, self.piece = trees, slot, piece
        self.send_sem, self.recv_sem = send_sem, recv_sem
        self.to = {1: plus, -1: minus, 0: pair}
        self.source = source

    def index(self, u, dz, h):
        return self.slot((4 - u) % 4 if h % 2 else u, dz)

    def ref(self, u, dz, h):
        return self.piece(self.index(u, dz, h), h)

    def copy(self, u, dz, h):
        su, sdz, step = self.trees[h][(u, dz)]
        here = there = self.ref(su, sdz, h)
        if self.source is not None and (su, sdz) == (0, 0):
            here = self.source(h, step)
        return pltpu.make_async_remote_copy(
            src_ref=here,
            dst_ref=there,
            send_sem=self.send_sem.at[h, u * 2 + dz],
            recv_sem=self.recv_sem.at[h, u * 2 + dz],
            device_id=self.to[-step if h % 2 else step],
            device_id_type=MESH,
        )

    def send(self, h, *targets):
        for u, dz in targets:
            self.copy(u, dz, h).start()

    def pass_on(self, u, dz, h):
        self.send(h, *[to for to, by in self.trees[h].items() if by[:2] == (u, dz)])

    def arrived(self, u, dz, h):
        ref = self.ref(u, dz, h)
        pltpu.make_async_remote_copy(
            src_ref=ref,
            dst_ref=ref,
            send_sem=self.send_sem.at[h, u * 2 + dz],
            recv_sem=self.recv_sem.at[h, u * 2 + dz],
            device_id=self.to[1],
            device_id_type=MESH,
        ).wait_recv()

    def sent(self):
        for h, tree in enumerate(self.trees):
            for u, dz in tree:
                self.copy(u, dz, h).wait_send()


class Across:
    def __init__(self, gather, piece, send_sem, recv_sem, core_pair):
        self.gather, self.piece = gather, piece
        self.send_sem, self.recv_sem, self.core_pair = send_sem, recv_sem, core_pair
        self.keys = [(0, 0), *OUT_TREE]

    def copy(self, u, dz, h, other):
        ref = self.piece(self.gather.index(u, dz, h), h, other)
        return pltpu.make_async_remote_copy(
            src_ref=ref, dst_ref=ref, send_sem=self.send_sem.at[h, u * 2 + dz], recv_sem=self.recv_sem.at[h, u * 2 + dz],
            device_id=self.core_pair, device_id_type=MESH,
        )

    def send(self, u, dz, h):
        self.copy(u, dz, h, False).start()

    def arrived(self, u, dz, h):
        self.copy(u, dz, h, True).wait_recv()

    def sent(self):
        for h in range(2):
            for u, dz in self.keys:
                self.copy(u, dz, h, False).wait_send()


def choose(i, values):
    result = values[-1]
    for n in range(len(values) - 2, -1, -1):
        result = jnp.where(i == n, values[n], result)
    return result


def kernel(
    hidden_ref, lengths_ref, gain_ref, wq_ref, wk_ref, wv_ref, wo_ref, qs_ref, ks_ref, vs_ref, os_ref,
    out_ref,
    nrm, raw_q, raw_k, raw_v, raw_o, snd, w_own, w_one, w_two, wo, len_t, acc_a, acc_b, acc_c, cos_t, sin_t, begin_t,
    q_t, kv_t, att_out, att, acc_o, ost, got,
    load_sem, a2a_s, a2a_r, one_s, one_r, core_s, core_r, rows_s, rows_r, ring_s, ring_r, racross_s, racross_r,
    one_in_s, one_in_r, two_in_s, two_in_r, o_s, o_r, att_s, att_r, across_s, across_r, fin_s, fin_r,
):
    f = lax.axis_index("fsdp")
    t = lax.axis_index("tp")
    x, zh = f // 2, f % 2
    y, zl, c = t // 4, (t // 2) % 2, t % 2
    rz = (zl + zh) % 2
    role = y * 2 + rz
    hb = role * 2 + c

    def device(ff, tt):
        return {"fsdp": ff, "tp": tt}

    x_plus = device(((x + 1) % 4) * 2 + zh, t)
    x_minus = device(((x + 3) % 4) * 2 + zh, t)
    z_pair = device(x * 2 + 1 - zh, y * 4 + (1 - zl) * 2 + c)
    y_plus = device(f, ((y + 1) % 4) * 4 + zl * 2 + c)
    y_minus = device(f, ((y + 3) % 4) * 4 + zl * 2 + c)
    zl_pair = device(f, y * 4 + (1 - zl) * 2 + c)
    core_pair = device(f, y * 4 + zl * 2 + 1 - c)

    barrier = pltpu.get_barrier_semaphore()
    for other in (x_plus, x_minus, z_pair):
        pl.semaphore_signal(barrier, inc=1, device_id=other, device_id_type=MESH)

    @pl.loop(1, 16)
    def _(i):
        pl.semaphore_signal(barrier, inc=1, device_id=device(f, (t + i) % 16), device_id_type=MESH)

    loads = [
        pltpu.make_async_copy(src, dst, load_sem.at[n])
        for n, (src, dst) in enumerate([(wo_ref, raw_o), (wq_ref, raw_q), (wk_ref, raw_k), (wv_ref, raw_v)])
    ]
    for j in range(8):
        loads.append(pltpu.make_async_copy(hidden_ref.at[:, pl.ds(j * 1024, 1024)], nrm.at[0, j], load_sem.at[4 + j]))
    for load in loads:
        load.start()

    def quantize(weight, inverse):
        return jnp.clip(weight.astype(F32) * inverse, -SATURATE, SATURATE).astype(BF16)

    def fsdp_slot(dx, dz):
        return ((x + 4 - dx) % 4) * 2 + (zh + dz) % 2

    out_gather = Gather(
        [OUT_TREE] * 2 + [PAIR_TREE] * 2, fsdp_slot, lambda s, h: wo.at[s, pl.ds(h * 16, 16)], o_s, o_r,
        x_plus, x_minus, z_pair,
    )
    one_gather = Gather(
        [IN_TREE] * 2, fsdp_slot, lambda s, h: w_one.at[s, pl.ds(h * 512, 512)], one_in_s, one_in_r, x_plus, x_minus, z_pair,
        lambda h, step: w_own.at[pl.ds(h * 512, 512), pl.ds(128 if step else 256, 256)],
    )
    two_gather = Gather(
        [IN_TREE] * 2, fsdp_slot, lambda s, h: w_two.at[s, pl.ds(h * 512, 512)], two_in_s, two_in_r, x_plus, x_minus, z_pair,
        lambda h, step: w_own.at[pl.ds(h * 512, 512), pl.ds(0 if step else 512, 128)],
    )
    def chip_slot(dy, dz):
        return ((y + 4 - dy) % 4) * 2 + (zl + dz) % 2

    def row_piece(s, h, core):
        return nrm.at[1, s, pl.ds(h * 256, 256), pl.ds(pl.multiple_of(core * 512, 512), 512)]

    row_gather = Gather(
        [OUT_TREE] * 2, chip_slot, lambda s, h: row_piece(s, h, c), ring_s, ring_r, y_plus, y_minus, zl_pair
    )
    row_across = Across(
        row_gather, lambda s, h, other: row_piece(s, h, 1 - c if other else c), racross_s, racross_r, core_pair
    )
    def att_slot(dy, dz):
        return ((y + 4 - dy) % 4) * 2 + (rz + dz) % 2

    def att_piece(s, core, half, n):
        return att.at[s, :, pl.ds(pl.multiple_of(core * 512 + half * 256 + n * 128, 128), 128)]

    att_gathers = [
        Gather(
            [OUT_TREE] * 2, att_slot, lambda s, h, n=n: att_piece(s, c, (zh + h) % 2, n),
            att_s.at[n], att_r.at[n], y_plus, y_minus, zl_pair,
        )
        for n in range(2)
    ]
    att_acrosses = [
        Across(
            att_gathers[n], lambda s, h, other, n=n: att_piece(s, 1 - c if other else c, (zh + h) % 2, n),
            across_s.at[n], across_r.at[n], core_pair,
        )
        for n in range(2)
    ]

    loads[0].wait()
    chip_cols = pl.ds(pl.multiple_of((f * 8 + t // 2) * 128, 128), 128)
    chip_scale = jnp.broadcast_to(1.0 / os_ref[:, chip_cols], (128, 128))
    on_diagonal = lax.broadcasted_iota(jnp.int32, (128, 128), 0) == lax.broadcasted_iota(jnp.int32, (128, 128), 1)
    chip_column = jnp.sum(jnp.where(on_diagonal, chip_scale, 0.0), axis=1, keepdims=True)
    own_scale = jnp.where(c == 0, chip_column[:64], chip_column[64:])

    @pl.loop(0, 16)
    def _(i):
        cols = pl.ds(pl.multiple_of(i * 512, 512), 512)
        wo[f, :, cols] = quantize(raw_o[:, cols], own_scale)

    pl.semaphore_wait(barrier, 18)
    for place in ((1, 0), (3, 0)):
        for h in range(4):
            out_gather.send(h, place)
    for h in range(2):
        out_gather.send(h, (0, 1))

    for load in loads[1:4]:
        load.wait()

    @pl.loop(0, 8)
    def _(r):
        for n in range(2):
            for part, head, place in ((zh, 1, 0), (zh, 0, 128), (1 - zh, 0, 384), (1 - zh, 1, 512)):
                cols = pl.ds(pl.multiple_of((r * 2 + n) * 512 + part * 256 + head * 128, 128), 128)
                snd[r * 2 + n, :, place:place + 128] = quantize(raw_q[:, cols], 1.0 / qs_ref[:, cols])
        cols = pl.ds(pl.multiple_of(r * 128, 128), 128)
        snd[r * 2, :, 256:384] = quantize(raw_k[:, cols], 1.0 / ks_ref[:, cols])
        snd[r * 2 + 1, :, 256:384] = quantize(raw_v[:, cols], 1.0 / vs_ref[:, cols])

    for n in range(8):
        len_t[0, n:n + 1, :] = jnp.full((1, 128), lengths_ref[0, n], jnp.int32)

    def block_copy(i):
        to = (t + i) % 16
        block = ((to // 4) * 2 + ((to // 2) % 2 + zh) % 2) * 2 + to % 2
        return pltpu.make_async_remote_copy(
            src_ref=snd.at[block],
            dst_ref=w_own.at[pl.ds(pl.multiple_of(t * 64, 64), 64)],
            send_sem=a2a_s.at[i],
            recv_sem=a2a_r.at[i],
            device_id=device(f, to),
            device_id_type=MESH,
        )

    @pl.loop(1, 16)
    def _(i):
        block_copy(i).start()

    w_own[pl.ds(pl.multiple_of(t * 64, 64), 64)] = snd[hb]

    def one_copy(n, src, dst, device_id):
        return pltpu.make_async_remote_copy(
            src_ref=src, dst_ref=dst, send_sem=one_s.at[n], recv_sem=one_r.at[n],
            device_id=device_id, device_id_type=MESH,
        )

    len_copy = one_copy(0, len_t.at[0], len_t.at[1], z_pair)
    len_copy.start()

    for load in loads[4:]:
        load.wait()

    def row_copy(h, chip):
        rows, cols = pl.ds(h * 256, 256), pl.ds(pl.multiple_of(c * 512, 512), 512)
        return pltpu.make_async_remote_copy(
            src_ref=nrm.at[0, chip, rows, cols], dst_ref=nrm.at[1, chip, rows, cols],
            send_sem=rows_s.at[h], recv_sem=rows_r.at[h], device_id=z_pair, device_id_type=MESH,
        )

    for h in range(2):
        @pl.loop(h * 16, h * 16 + 16)
        def _(i):
            rows = pl.ds(pl.multiple_of(i * 16, 16), 16)
            square = jnp.zeros((16, 1024), F32)
            for j in range(8):
                wide = nrm[0, j, rows, :].astype(F32)
                square += wide * wide
            inverse = lax.rsqrt(jnp.sum(square, axis=1, keepdims=True) * (1.0 / D) + EPSILON)
            for j in range(8):
                wide = nrm[0, j, rows, :].astype(F32)
                nrm[0, j, rows, :] = (wide * inverse * gain_ref[:, j * 1024:(j + 1) * 1024]).astype(BF16)

        row_copy(h, y * 2 + 1 - zl).start()

    place = lax.broadcasted_iota(jnp.int32, (TOK, 128), 0)
    lane = lax.broadcasted_iota(jnp.int32, (TOK, 128), 1)

    def tables(replica):
        begin = jnp.zeros((TOK, 128), jnp.int32)
        start = jnp.zeros((1, 128), jnp.int32)
        for n in range(8):
            begin = jnp.where(place >= start, start, begin)
            start = start + len_t[replica, n:n + 1, :]
        begin_t[replica] = begin
        frequency = jnp.exp((lane % 64).astype(F32) * (-2.0 * math.log(ROPE_BASE) / HD))
        angle = (place - begin).astype(F32) * frequency
        cos_t[replica] = jnp.cos(angle)
        sine = jnp.sin(angle)
        sin_t[replica] = jnp.where(lane < 64, -sine, sine)

    tables(0)
    len_copy.wait_recv()
    tables(1)

    def row_take(h):
        row_copy(h, y * 2 + zl).wait_recv()
        row_gather.send(h, (1, 0), (0, 1))
        row_across.send(0, 0, h)

    def row_wait(u, dz):
        for h in range(2):
            row_gather.arrived(u, dz, h)
            row_gather.pass_on(u, dz, h)
            row_across.send(u, dz, h)

    row_take(0)

    for h in range(2):
        @pl.loop(h * 8, h * 8 + 8)
        def _(src):
            @pl.when(src != t)
            def _():
                ref = w_own.at[pl.ds(pl.multiple_of(src * 64, 64), 64)]
                i = (t + 16 - src) % 16
                pltpu.make_async_remote_copy(
                    src_ref=ref, dst_ref=ref, send_sem=a2a_s.at[i], recv_sem=a2a_r.at[i],
                    device_id=core_pair, device_id_type=MESH,
                ).wait_recv()

    def open_with(gather, *places):
        for place in places:
            for h in range(2):
                gather.send(h, place)

    open_with(one_gather, (1, 0), (0, 1), (3, 0))
    open_with(two_gather, (0, 1))
    for h in range(2, 4):
        out_gather.send(h, (0, 1))
    row_take(1)
    open_with(row_gather, (3, 0))

    for total in (acc_a, acc_b, acc_c):
        total[...] = jnp.zeros_like(total)

    def project(gather, replica, places):
        for dz in range(2):
            some = [(u, h) for u, z in places for h in range(2) if z == dz and (u, z) != (0, 0)]
            if not some:
                continue
            slots, halves = [gather.index(u, dz, h) for u, h in some], [h for _, h in some]
            weight, total = (w_one, (acc_a, acc_b)[dz]) if gather is one_gather else (w_two, acc_c)

            @pl.loop(0, len(some))
            def _(i):
                s, h = choose(i, slots), choose(i, halves)
                cols = pl.ds(pl.multiple_of(h * 512, 512), 512)
                total[replica] += jnp.dot(nrm[replica, s, :, cols], weight[s, cols, :], preferred_element_type=F32)

        if (0, 0) in places:
            lanes, total = (slice(128, 384), acc_a) if gather is one_gather else (slice(0, 128), acc_c)

            @pl.loop(0, 2)
            def _(h):
                cols = pl.ds(pl.multiple_of(h * 512, 512), 512)
                total[replica] += jnp.dot(nrm[replica, f, :, cols], w_own[cols, lanes], preferred_element_type=F32)

    def wait(gather, *places):
        for u, dz in places:
            for h in range(len(gather.trees)):
                gather.arrived(u, dz, h)

    def relay(gather, u, dz):
        for h in range(len(gather.trees)):
            gather.arrived(u, dz, h)
            if dz == 0:
                gather.pass_on(u, dz, h)
        if dz == 1 and u == 0:
            for place in ((1, 1), (3, 1)):
                for h, tree in enumerate(gather.trees):
                    if tree[place][:2] == (0, 1):
                        gather.send(h, place)
        elif dz == 1:
            for h in range(len(gather.trees)):
                gather.pass_on(u, dz, h)

    project(one_gather, 0, [(0, 0)])
    row_wait(1, 0)
    relay(one_gather, 1, 0)
    project(one_gather, 0, [(1, 0)])
    row_wait(0, 1)
    relay(one_gather, 0, 1)
    wait(one_gather, (3, 0))
    project(one_gather, 0, [(0, 1), (3, 0)])
    row_wait(3, 0)
    row_wait(2, 0)
    wait(one_gather, (2, 0))
    project(one_gather, 0, [(2, 0)])
    row_wait(1, 1)
    row_wait(3, 1)
    relay(one_gather, 1, 1)
    project(one_gather, 0, [(1, 1)])
    row_wait(2, 1)
    for h in range(2):
        for u in range(4):
            for dz in range(2):
                row_across.arrived(u, dz, h)
    relay(out_gather, 1, 0)
    project(one_gather, 1, [(0, 0), (1, 0), (3, 0)])
    wait(one_gather, (3, 1))
    open_with(two_gather, (1, 0), (3, 0))
    relay(two_gather, 0, 1)
    project(one_gather, 0, [(3, 1)])
    project(one_gather, 1, [(2, 0), (0, 1), (1, 1), (3, 1)])
    wait(one_gather, (2, 1))
    for replica in (1, 0):
        project(one_gather, replica, [(2, 1)])

    def rope(v, replica):
        return v * cos_t[replica] + pltpu.roll(v, 64, axis=1) * sin_t[replica]

    def core_copy(replica, core):
        return pltpu.make_async_remote_copy(
            src_ref=kv_t.at[replica, core], dst_ref=kv_t.at[replica, core],
            send_sem=core_s.at[replica], recv_sem=core_r.at[replica],
            device_id=core_pair, device_id_type=MESH,
        )

    kv_cols = pl.ds(pl.multiple_of(role * 128, 128), 128)
    for replica in (1, 0):
        product = acc_a[replica, :, 128:256] + acc_b[replica, :, 0:128]
        key_raw = (product * ks_ref[:, kv_cols]).astype(BF16).astype(F32)
        value = product * vs_ref[:, kv_cols]
        kv_t[replica, c] = jnp.where(c == 0, rope(key_raw, replica), value).astype(BF16)
        core_copy(replica, c).start()

    def query(replica, n):
        product = acc_c[replica] if n else acc_a[replica, :, 0:128] + acc_b[replica, :, 128:256]
        scale = qs_ref[:, pl.ds(pl.multiple_of(hb * 512 + zh * 256 + n * 128, 128), 128)]
        q_t[replica, n] = rope(product * scale, replica).astype(BF16)

    def attend(replica, n, out):
        query(replica, n)
        for b in range(4):
            first = max(0, b * 128 - 256)
            width = (b + 1) * 128 - first
            rows = slice(b * 128, (b + 1) * 128)
            keys = slice(first, first + width)
            scores = lax.dot_general(
                q_t[replica, n, rows], kv_t[replica, 0, keys], (((1,), (1,)), ((), ())), preferred_element_type=F32
            ) * HD ** (-0.5)
            p = lax.broadcasted_iota(jnp.int32, (128, width), 0) + b * 128
            s = lax.broadcasted_iota(jnp.int32, (128, width), 1) + first
            keep = (s <= p) & (s >= begin_t[replica, rows, 0:1])
            scores = jnp.where(keep, scores, MASKED_SCORE)
            weights = jnp.exp(scores - jnp.max(scores, axis=1, keepdims=True))
            total = jnp.sum(weights, axis=1, keepdims=True)
            mixed = jnp.dot(weights.astype(BF16), kv_t[replica, 1, keys], preferred_element_type=F32)
            out[rows, :] = (mixed / total).astype(BF16)

    def att_copy(n):
        return one_copy(1 + n, att_out.at[n], att_piece(role, c, zh, n), z_pair)

    def att_arrived(n):
        one_copy(1 + n, att_out.at[n], att_piece(role, c, 1 - zh, n), z_pair).wait_recv()
        att_gathers[n].pass_on(0, 0, 1)
        att_acrosses[n].send(0, 0, 1)

    def att_own(n):
        attend(0, n, att_piece(role, c, zh, n))
        att_gathers[n].pass_on(0, 0, 0)
        att_acrosses[n].send(0, 0, 0)

    def take(n, *places):
        for u, dz in places:
            for h in range(2):
                att_gathers[n].arrived(u, dz, h)
                att_gathers[n].pass_on(u, dz, h)
                att_acrosses[n].send(u, dz, h)

    core_copy(1, 1 - c).wait_recv()
    attend(1, 0, att_out.at[0])
    att_copy(0).start()
    relay(out_gather, 3, 0)
    core_copy(0, 1 - c).wait_recv()
    att_own(0)
    att_arrived(0)
    relay(two_gather, 1, 0)
    for h in range(4):
        out_gather.arrived(2, 0, h)
    for h in range(2):
        out_gather.send(h, (2, 1))
    take(0, (1, 0), (0, 1))
    relay(two_gather, 1, 1)
    for replica in (1, 0):
        project(two_gather, replica, [(0, 0), (1, 0), (0, 1), (1, 1)])
    take(0, (3, 0), (2, 0))
    wait(two_gather, (3, 0), (2, 0), (3, 1))
    relay(out_gather, 0, 1)
    for replica in (1, 0):
        project(two_gather, replica, [(3, 0), (2, 0), (3, 1)])
    take(0, (1, 1), (3, 1), (2, 1))
    wait(two_gather, (2, 1))
    for replica in (1, 0):
        project(two_gather, replica, [(2, 1)])
    attend(1, 1, att_out.at[1])
    att_copy(1).start()
    for h in range(2, 4):
        out_gather.send(h, (2, 1))
    att_own(1)
    att_arrived(1)

    early = [fsdp_slot(dx, dz) for dx, dz in ((0, 0), (1, 0), (3, 0), (0, 1))]
    late = [fsdp_slot(dx, dz) for dx, dz in ((2, 0), (1, 1), (3, 1), (2, 1))]

    def mix_head(n, *places):
        for u, dz in places:
            for h in range(2):
                att_acrosses[n].arrived(u, dz, h)
        roles = [att_slot(u, dz) for u, dz in places]

        @pl.loop(0, len(roles))
        def _(i):
            r = choose(i, roles)
            left = jnp.concatenate([att[r, :, k * 256 + n * 128:k * 256 + n * 128 + 128] for k in range(4)], axis=1)
            cols = [pl.ds(pl.multiple_of(r * 1024 + k * 256 + n * 128, 128), 128) for k in range(4)]
            right = jnp.concatenate(
                [jnp.concatenate([wo[s, :, k] for k in cols], axis=1) for s in early], axis=0
            )
            acc_o[0] += lax.dot_general(left, right, (((1,), (1,)), ((), ())), preferred_element_type=F32)

    def mix_late():
        @pl.loop(0, 8)
        def _(r):
            cols = pl.ds(pl.multiple_of(r * 1024, 1024), 1024)
            right = jnp.concatenate([wo[s, :, cols] for s in late], axis=0)
            acc_o[1] += lax.dot_general(att[r], right, (((1,), (1,)), ((), ())), preferred_element_type=F32)

    def finish(which):
        ost[which] = acc_o[which].astype(BF16)

        @pl.loop(1, 16)
        def _(i):
            final_copy(which, i).start()

        got[which, t] = ost[which, pl.ds(pl.multiple_of(t * 32, 32), 32)]

    def final_copy(which, i):
        to = (t + i) % 16
        return pltpu.make_async_remote_copy(
            src_ref=ost.at[which, pl.ds(pl.multiple_of(to * 32, 32), 32)],
            dst_ref=got.at[which, t],
            send_sem=fin_s.at[which, i],
            recv_sem=fin_r.at[which, i],
            device_id=device(f, to),
            device_id_type=MESH,
        )

    acc_o[...] = jnp.zeros_like(acc_o)
    ring = [(0, 0), (1, 0), (3, 0), (2, 0)]
    beyond = [(0, 1), (1, 1), (3, 1), (2, 1)]
    mix_head(0, *ring)
    take(1, (1, 0), (0, 1))
    mix_head(0, *beyond)
    take(1, (3, 0), (2, 0))
    mix_head(1, *ring)
    take(1, (1, 1), (3, 1), (2, 1))
    mix_head(1, *beyond)
    finish(0)
    wait(out_gather, (1, 1), (3, 1), (2, 1))
    mix_late()
    finish(1)

    def collect(which, offsets):
        @pl.loop(1, 16)
        def _(i):
            ref = got.at[which, (t + 16 - i) % 16]
            pltpu.make_async_remote_copy(
                src_ref=ref, dst_ref=ref, send_sem=fin_s.at[which, i], recv_sem=fin_r.at[which, i],
                device_id=core_pair, device_id_type=MESH,
            ).wait_recv()

        @pl.loop(0, 8)
        def _(k):
            for n, (dx, dz) in enumerate(offsets):
                chip = (k // 2) * 2 + (k % 2 + dz) % 2
                cols = pl.ds(pl.multiple_of((fsdp_slot(dx, dz) * 8 + chip) * 128, 128), 128)
                part = slice(n * 64, (n + 1) * 64)
                both = jnp.concatenate([got[which, k * 2, :, part], got[which, k * 2 + 1, :, part]], axis=1)
                out_ref[:, cols] = (both.astype(F32) * os_ref[:, cols]).astype(BF16)

    collect(0, ((0, 0), (1, 0), (3, 0), (0, 1)))
    collect(1, ((2, 0), (1, 1), (3, 1), (2, 1)))

    @pl.loop(1, 16)
    def _(i):
        block_copy(i).wait_send()
        final_copy(0, i).wait_send()
        final_copy(1, i).wait_send()

    len_copy.wait_send()
    att_copy(0).wait_send()
    att_copy(1).wait_send()
    for n in range(2):
        core_copy(n, c).wait_send()
        row_copy(n, y * 2 + 1 - zl).wait_send()
    for group in (out_gather, one_gather, two_gather, row_gather, row_across, *att_gathers, *att_acrosses):
        group.sent()


def shards(
    hidden_in, lengths, norm_gain, query_weight, key_weight, value_weight, out_weight,
    query_scale, key_scale, value_scale, out_scale,
):
    vmem = pl.BlockSpec(memory_space=pltpu.VMEM)
    any_space = pl.BlockSpec(memory_space=pl.ANY)
    smem = pl.BlockSpec(memory_space=pltpu.SMEM)
    dma = pltpu.SemaphoreType.DMA
    return pl.pallas_call(
        kernel,
        out_shape=jax.ShapeDtypeStruct((32, D), BF16),
        in_specs=[any_space, smem, vmem, any_space, any_space, any_space, any_space, vmem, vmem, vmem, vmem],
        out_specs=vmem,
        scratch_shapes=[
            pltpu.VMEM((2, 8, TOK, 1024), BF16),
            pltpu.VMEM((64, D), BF16),
            pltpu.VMEM((64, 1024), BF16),
            pltpu.VMEM((64, 1024), BF16),
            pltpu.VMEM((64, D), BF16),
            pltpu.VMEM((16, 64, 640), BF16),
            pltpu.VMEM((1024, 640), BF16),
            pltpu.VMEM((8, 1024, 256), BF16),
            pltpu.VMEM((8, 1024, 128), BF16),
            pltpu.VMEM((8, 64, D), BF16),
            pltpu.VMEM((2, 8, 128), jnp.int32),
            pltpu.VMEM((2, TOK, 256), F32),
            pltpu.VMEM((2, TOK, 256), F32),
            pltpu.VMEM((2, TOK, HD), F32),
            pltpu.VMEM((2, TOK, HD), F32),
            pltpu.VMEM((2, TOK, HD), F32),
            pltpu.VMEM((2, TOK, HD), jnp.int32),
            pltpu.VMEM((2, 2, TOK, HD), BF16),
            pltpu.VMEM((2, 2, TOK, HD), BF16),
            pltpu.VMEM((2, TOK, HD), BF16),
            pltpu.VMEM((8, TOK, 1024), BF16),
            pltpu.VMEM((2, TOK, 256), F32),
            pltpu.VMEM((2, TOK, 256), BF16),
            pltpu.VMEM((2, 16, 32, 256), BF16),
            dma((12,)), dma((16,)), dma((16,)), dma((3,)), dma((3,)), dma((2,)), dma((2,)), dma((2,)), dma((2,)),
            dma((2, 8)), dma((2, 8)), dma((2, 8)), dma((2, 8)),
            dma((2, 8)), dma((2, 8)), dma((2, 8)), dma((2, 8)), dma((4, 8)), dma((4, 8)),
            dma((2, 2, 8)), dma((2, 2, 8)), dma((2, 2, 8)), dma((2, 2, 8)),
            dma((2, 16)), dma((2, 16)),
        ],
        compiler_params=pltpu.CompilerParams(
            collective_id=0, has_side_effects=True, vmem_limit_bytes=60 * 1024 * 1024
        ),
        cost_estimate=pl.CostEstimate(flops=10_000_000_000, bytes_accessed=16_000_000, transcendentals=1_000_000),
        name="refresh_and_prefill",
    )(
        hidden_in, lengths, norm_gain.reshape(1, -1), query_weight, key_weight, value_weight, out_weight.T,
        query_scale.reshape(1, -1), key_scale.reshape(1, -1), value_scale.reshape(1, -1), out_scale.reshape(1, -1),
    )


def solution(mesh):
    in_specs = (
        P("fsdp", None),
        P("fsdp", None),
        P(),
        P(("fsdp", "tp"), None),
        P(("fsdp", "tp"), None),
        P(("fsdp", "tp"), None),
        P(None, ("fsdp", "tp")),
        P(),
        P(),
        P(),
        P(),
    )
    return jax.shard_map(
        shards, mesh=mesh, in_specs=in_specs, out_specs=P(("fsdp", "tp"), None), check_vma=False
    )
```

time: 153 us -> 141 us (0.922)
  Pallas kernels: 151 us -> 139 us
    pallas_call x1, Pallas kernels: 151 us -> 139 us  [shards(): pl.pallas_call(kernel, out_shape=jax.ShapeDtypeStruct((32, D), BF16), in_...]
where the time goes in v3:
time: 141 us
  Pallas kernels  139 us (99%)
  local copies, waits for them, and re-layouts  1.87 us (1%)
    pallas_call x1, Pallas kernels, shards(): pl.pallas_call(kernel, out_shape=jax.ShapeDtypeStruct((32, D), BF16), in_...  139 us

profile of v3, /device:TPU:1, one launch (start us, length us, event | category | flops | bytes accessed | tf_op | source)
XLA Modules:
  0.0 141.2 jit_solution(4617099037509257066)
XLA Ops:
  0.0 139.3 %refresh_and_prefill.1 = bf16[32,8192]{1,0:T(8,128)(2,1)} custom-call(bf16[512,8192]{1,0:T(8,128)(2,1)} %hidden_ref.1, s32[1,8]{1,0:T(1,128)} %lengths_ref.1, f32[1,8192]{1,0:T(1,128)} %bitcast.7, bf16[64,8192]{1,0:T(8,128)(2,1)} %wq_ref.1, bf16[64,1024]{1,0:T(8,128)(2,1)} %wk_ref.1, bf16[64,1024]{1,0:T(8,128)(2,1)} %wv_ref.1, bf16[64,8192]{1,0:T(8,128)(2,1)} %bitcast.6, ...), custom_call_target="tpu_custom_call" | custom-call | flops 10000000000 | bytes 16000000 | tf_op jit(solution)/shard_map/refresh_and_prefill/pallas_call | solution.py:633
  139.3 1.9 %copy.13 = bf16[32,8192]{1,0:T(8,128)(2,1)} copy(bf16[32,8192]{1,0:T(8,128)(2,1)} %refresh_and_prefill.1) | data formatting | bytes 1048576

commit v4 on v3

--- a/solution.py
+++ b/solution.py
@@ -226,8 +226,7 @@
     for place in ((1, 0), (3, 0)):
         for h in range(4):
             out_gather.send(h, place)
-    for h in range(2):
-        out_gather.send(h, (0, 1))
+    out_gather.send(0, (0, 1))
 
     for load in loads[1:4]:
         load.wait()
@@ -349,7 +348,7 @@
 
     open_with(one_gather, (1, 0), (0, 1), (3, 0))
     open_with(two_gather, (0, 1))
-    for h in range(2, 4):
+    for h in range(1, 4):
         out_gather.send(h, (0, 1))
     row_take(1)
     open_with(row_gather, (3, 0))
@@ -378,6 +377,28 @@
             def _(h):
                 cols = pl.ds(pl.multiple_of(h * 512, 512), 512)
                 total[replica] += jnp.dot(nrm[replica, f, :, cols], w_own[cols, lanes], preferred_element_type=F32)
+
+    def project_items(gather, replicas, places):
+        first = gather is one_gather
+        for dz in range(2):
+            slots = [fsdp_slot(u, z) for u, z in places if z == dz and (u, z) != (0, 0)]
+            if not slots:
+                continue
+            weight, total = (w_one, (acc_a, acc_b)[dz]) if first else (w_two, acc_c)
+
+            @pl.loop(0, len(slots) * len(replicas))
+            def _(i):
+                s = choose(i % len(slots), slots)
+                replica = choose(i // len(slots), replicas)
+                total[replica] += jnp.dot(nrm[replica, s], weight[s], preferred_element_type=F32)
+
+        if (0, 0) in places:
+            lanes, total = (slice(128, 384), acc_a) if first else (slice(0, 128), acc_c)
+
+            @pl.loop(0, len(replicas))
+            def _(i):
+                replica = choose(i, replicas)
+                total[replica] += jnp.dot(nrm[replica, f], w_own[:, lanes], preferred_element_type=F32)
 
     def wait(gather, *places):
         for u, dz in places:
@@ -398,6 +419,11 @@
             for h in range(len(gather.trees)):
                 gather.pass_on(u, dz, h)
 
+    def out_relay(u, dz, *parts):
+        for h in parts:
+            out_gather.arrived(u, dz, h)
+            out_gather.pass_on(u, dz, h)
+
     project(one_gather, 0, [(0, 0)])
     row_wait(1, 0)
     relay(one_gather, 1, 0)
@@ -410,25 +436,26 @@
     row_wait(2, 0)
     wait(one_gather, (2, 0))
     project(one_gather, 0, [(2, 0)])
+    relay(one_gather, 1, 1)
+    out_relay(1, 0, 0, 1)
+    for h in range(4):
+        out_gather.arrived(3, 0, h)
+    out_gather.pass_on(3, 0, 2)
+    project(one_gather, 0, [(1, 1)])
     row_wait(1, 1)
+    wait(one_gather, (3, 1))
+    open_with(two_gather, (1, 0), (3, 0))
+    relay(two_gather, 0, 1)
+    project(one_gather, 0, [(3, 1)])
     row_wait(3, 1)
-    relay(one_gather, 1, 1)
-    project(one_gather, 0, [(1, 1)])
     row_wait(2, 1)
     for h in range(2):
         for u in range(4):
             for dz in range(2):
                 row_across.arrived(u, dz, h)
-    relay(out_gather, 1, 0)
-    project(one_gather, 1, [(0, 0), (1, 0), (3, 0)])
-    wait(one_gather, (3, 1))
-    open_with(two_gather, (1, 0), (3, 0))
-    relay(two_gather, 0, 1)
-    project(one_gather, 0, [(3, 1)])
-    project(one_gather, 1, [(2, 0), (0, 1), (1, 1), (3, 1)])
+    project_items(one_gather, (1,), [(0, 0), (1, 0), (3, 0), (2, 0), (0, 1), (1, 1), (3, 1)])
     wait(one_gather, (2, 1))
-    for replica in (1, 0):
-        project(one_gather, replica, [(2, 1)])
+    project_items(one_gather, (1, 0), [(2, 1)])
 
     def rope(v, replica):
         return v * cos_t[replica] + pltpu.roll(v, 64, axis=1) * sin_t[replica]
@@ -495,32 +522,25 @@
     core_copy(1, 1 - c).wait_recv()
     attend(1, 0, att_out.at[0])
     att_copy(0).start()
-    relay(out_gather, 3, 0)
+    out_gather.pass_on(3, 0, 3)
     core_copy(0, 1 - c).wait_recv()
     att_own(0)
     att_arrived(0)
     relay(two_gather, 1, 0)
-    for h in range(4):
-        out_gather.arrived(2, 0, h)
-    for h in range(2):
-        out_gather.send(h, (2, 1))
+    out_relay(2, 0, 0, 1)
     take(0, (1, 0), (0, 1))
     relay(two_gather, 1, 1)
-    for replica in (1, 0):
-        project(two_gather, replica, [(0, 0), (1, 0), (0, 1), (1, 1)])
+    out_relay(1, 0, 2, 3)
+    relay(out_gather, 0, 1)
+    project_items(two_gather, (1, 0), [(0, 0), (0, 1)])
     take(0, (3, 0), (2, 0))
     wait(two_gather, (3, 0), (2, 0), (3, 1))
-    relay(out_gather, 0, 1)
-    for replica in (1, 0):
-        project(two_gather, replica, [(3, 0), (2, 0), (3, 1)])
+    project_items(two_gather, (1, 0), [(1, 0), (3, 0), (2, 0), (1, 1), (3, 1)])
     take(0, (1, 1), (3, 1), (2, 1))
     wait(two_gather, (2, 1))
-    for replica in (1, 0):
-        project(two_gather, replica, [(2, 1)])
+    project_items(two_gather, (1, 0), [(2, 1)])
     attend(1, 1, att_out.at[1])
     att_copy(1).start()
-    for h in range(2, 4):
-        out_gather.send(h, (2, 1))
     att_own(1)
     att_arrived(1)
 
@@ -575,6 +595,7 @@
     beyond = [(0, 1), (1, 1), (3, 1), (2, 1)]
     mix_head(0, *ring)
     take(1, (1, 0), (0, 1))
+    out_relay(2, 0, 2, 3)
     mix_head(0, *beyond)
     take(1, (3, 0), (2, 0))
     mix_head(1, *ring)

time: 141 us -> 134 us (0.950)
  Pallas kernels: 139 us -> 132 us
    pallas_call x1, Pallas kernels: 139 us -> 132 us  [shards(): pl.pallas_call(kernel, out_shape=jax.ShapeDtypeStruct((32, D), BF16), in_...]
where the time goes in v4:
time: 134 us
  Pallas kernels  132 us (99%)
  local copies, waits for them, and re-layouts  1.87 us (1%)
    pallas_call x1, Pallas kernels, shards(): pl.pallas_call(kernel, out_shape=jax.ShapeDtypeStruct((32, D), BF16), in_...  132 us

profile of v4, /device:TPU:1, one launch (start us, length us, event | category | flops | bytes accessed | tf_op | source)
XLA Modules:
  0.0 133.8 jit_solution(10237264068927782164)
XLA Ops:
  0.0 132.0 %refresh_and_prefill.1 = bf16[32,8192]{1,0:T(8,128)(2,1)} custom-call(bf16[512,8192]{1,0:T(8,128)(2,1)} %hidden_ref.1, s32[1,8]{1,0:T(1,128)} %lengths_ref.1, f32[1,8192]{1,0:T(1,128)} %bitcast.7, bf16[64,8192]{1,0:T(8,128)(2,1)} %wq_ref.1, bf16[64,1024]{1,0:T(8,128)(2,1)} %wk_ref.1, bf16[64,1024]{1,0:T(8,128)(2,1)} %wv_ref.1, bf16[64,8192]{1,0:T(8,128)(2,1)} %bitcast.6, ...), custom_call_target="tpu_custom_call" | custom-call | flops 10000000000 | bytes 16000000 | tf_op jit(solution)/shard_map/refresh_and_prefill/pallas_call | solution.py:654
  132.0 1.9 %copy.13 = bf16[32,8192]{1,0:T(8,128)(2,1)} copy(bf16[32,8192]{1,0:T(8,128)(2,1)} %refresh_and_prefill.1) | data formatting | bytes 1048576

commit v5 on v4

--- a/solution.py
+++ b/solution.py
@@ -166,7 +166,7 @@
         return ((x + 4 - dx) % 4) * 2 + (zh + dz) % 2
 
     out_gather = Gather(
-        [OUT_TREE] * 2 + [PAIR_TREE] * 2, fsdp_slot, lambda s, h: wo.at[s, pl.ds(h * 16, 16)], o_s, o_r,
+        [OUT_TREE] * 4, fsdp_slot, lambda s, h: wo.at[s, pl.ds(h * 16, 16)], o_s, o_r,
         x_plus, x_minus, z_pair,
     )
     one_gather = Gather(
@@ -353,7 +353,7 @@
     row_take(1)
     open_with(row_gather, (3, 0))
 
-    for total in (acc_a, acc_b, acc_c):
+    for total in (acc_a, acc_b, acc_c, acc_o):
         total[...] = jnp.zeros_like(total)
 
     def project(gather, replica, places):
@@ -425,6 +425,7 @@
             out_gather.pass_on(u, dz, h)
 
     project(one_gather, 0, [(0, 0)])
+    project_items(two_gather, (0,), [(0, 0)])
     row_wait(1, 0)
     relay(one_gather, 1, 0)
     project(one_gather, 0, [(1, 0)])
@@ -447,6 +448,7 @@
     open_with(two_gather, (1, 0), (3, 0))
     relay(two_gather, 0, 1)
     project(one_gather, 0, [(3, 1)])
+    project_items(two_gather, (0,), [(0, 1)])
     row_wait(3, 1)
     row_wait(2, 1)
     for h in range(2):
@@ -519,6 +521,34 @@
                 att_gathers[n].pass_on(u, dz, h)
                 att_acrosses[n].send(u, dz, h)
 
+    early = [fsdp_slot(dx, dz) for dx, dz in ((0, 0), (1, 0), (3, 0), (0, 1))]
+    late = [fsdp_slot(dx, dz) for dx, dz in ((2, 0), (1, 1), (3, 1), (2, 1))]
+
+    def mix_head(n, *places):
+        for u, dz in places:
+            for h in range(2):
+                att_acrosses[n].arrived(u, dz, h)
+        roles = [att_slot(u, dz) for u, dz in places]
+
+        @pl.loop(0, len(roles))
+        def _(i):
+            r = choose(i, roles)
+            left = jnp.concatenate([att[r, :, k * 256 + n * 128:k * 256 + n * 128 + 128] for k in range(4)], axis=1)
+            cols = [pl.ds(pl.multiple_of(r * 1024 + k * 256 + n * 128, 128), 128) for k in range(4)]
+            right = jnp.concatenate(
+                [jnp.concatenate([wo[s, :, k] for k in cols], axis=1) for s in early], axis=0
+            )
+            acc_o[0] += lax.dot_general(left, right, (((1,), (1,)), ((), ())), preferred_element_type=F32)
+
+    def mix_late():
+        @pl.loop(0, 8)
+        def _(r):
+            cols = pl.ds(pl.multiple_of(r * 1024, 1024), 1024)
+            right = jnp.concatenate([wo[s, :, cols] for s in late], axis=0)
+            acc_o[1] += lax.dot_general(att[r], right, (((1,), (1,)), ((), ())), preferred_element_type=F32)
+
+    ring = [(0, 0), (1, 0), (3, 0), (2, 0)]
+    beyond = [(0, 1), (1, 1), (3, 1), (2, 1)]
     core_copy(1, 1 - c).wait_recv()
     attend(1, 0, att_out.at[0])
     att_copy(0).start()
@@ -532,7 +562,7 @@
     relay(two_gather, 1, 1)
     out_relay(1, 0, 2, 3)
     relay(out_gather, 0, 1)
-    project_items(two_gather, (1, 0), [(0, 0), (0, 1)])
+    project_items(two_gather, (1,), [(0, 0), (0, 1)])
     take(0, (3, 0), (2, 0))
     wait(two_gather, (3, 0), (2, 0), (3, 1))
     project_items(two_gather, (1, 0), [(1, 0), (3, 0), (2, 0), (1, 1), (3, 1)])
@@ -542,33 +572,8 @@
     attend(1, 1, att_out.at[1])
     att_copy(1).start()
     att_own(1)
+    mix_head(0, *ring)
     att_arrived(1)
-
-    early = [fsdp_slot(dx, dz) for dx, dz in ((0, 0), (1, 0), (3, 0), (0, 1))]
-    late = [fsdp_slot(dx, dz) for dx, dz in ((2, 0), (1, 1), (3, 1), (2, 1))]
-
-    def mix_head(n, *places):
-        for u, dz in places:
-            for h in range(2):
-                att_acrosses[n].arrived(u, dz, h)
-        roles = [att_slot(u, dz) for u, dz in places]
-
-        @pl.loop(0, len(roles))
-        def _(i):
-            r = choose(i, roles)
-            left = jnp.concatenate([att[r, :, k * 256 + n * 128:k * 256 + n * 128 + 128] for k in range(4)], axis=1)
-            cols = [pl.ds(pl.multiple_of(r * 1024 + k * 256 + n * 128, 128), 128) for k in range(4)]
-            right = jnp.concatenate(
-                [jnp.concatenate([wo[s, :, k] for k in cols], axis=1) for s in early], axis=0
-            )
-            acc_o[0] += lax.dot_general(left, right, (((1,), (1,)), ((), ())), preferred_element_type=F32)
-
-    def mix_late():
-        @pl.loop(0, 8)
-        def _(r):
-            cols = pl.ds(pl.multiple_of(r * 1024, 1024), 1024)
-            right = jnp.concatenate([wo[s, :, cols] for s in late], axis=0)
-            acc_o[1] += lax.dot_general(att[r], right, (((1,), (1,)), ((), ())), preferred_element_type=F32)
 
     def finish(which):
         ost[which] = acc_o[which].astype(BF16)
@@ -590,10 +595,6 @@
             device_id_type=MESH,
         )
 
-    acc_o[...] = jnp.zeros_like(acc_o)
-    ring = [(0, 0), (1, 0), (3, 0), (2, 0)]
-    beyond = [(0, 1), (1, 1), (3, 1), (2, 1)]
-    mix_head(0, *ring)
     take(1, (1, 0), (0, 1))
     out_relay(2, 0, 2, 3)
     mix_head(0, *beyond)

time: 134 us -> 134 us (level)
  no operation moved by 1% of the time
where the time goes in v5:
time: 134 us; the launch traced here: 133 us
  Pallas kernels  131 us (98%)
  local copies, waits for them, and re-layouts  1.87 us (1%)
    pallas_call x1, Pallas kernels, shards(): pl.pallas_call(kernel, out_shape=jax.ShapeDtypeStruct((32, D), BF16), in_...  131 us

profile of v5, /device:TPU:1, one launch (start us, length us, event | category | flops | bytes accessed | tf_op | source)
XLA Modules:
  0.0 133.4 jit_solution(1794568118235002995)
XLA Ops:
  0.0 131.5 %refresh_and_prefill.1 = bf16[32,8192]{1,0:T(8,128)(2,1)} custom-call(bf16[512,8192]{1,0:T(8,128)(2,1)} %hidden_ref.1, s32[1,8]{1,0:T(1,128)} %lengths_ref.1, f32[1,8192]{1,0:T(1,128)} %bitcast.7, bf16[64,8192]{1,0:T(8,128)(2,1)} %wq_ref.1, bf16[64,1024]{1,0:T(8,128)(2,1)} %wk_ref.1, bf16[64,1024]{1,0:T(8,128)(2,1)} %wv_ref.1, bf16[64,8192]{1,0:T(8,128)(2,1)} %bitcast.6, ...), custom_call_target="tpu_custom_call" | custom-call | flops 10000000000 | bytes 16000000 | tf_op jit(solution)/shard_map/refresh_and_prefill/pallas_call | solution.py:655
  131.5 1.9 %copy.13 = bf16[32,8192]{1,0:T(8,128)(2,1)} copy(bf16[32,8192]{1,0:T(8,128)(2,1)} %refresh_and_prefill.1) | data formatting | bytes 1048576
